TPU v7x, 512 devices: a whole 4x8x8 slice. The times are simulated.
512 devices in a mesh: dp: 32 (over z_lo, y), tensor: 16 (over x, z_hi, core).
Axes of the slice: x: 4, y: 8, z: 8 (z_hi: 2, z_lo: 4; z = z_hi * 4 + z_lo), core: 2. Of those that a mesh axis runs over, the one named last changes fastest.
Arguments:
- grads: bfloat16 [32, 1536, 16384], P('dp', None, 'tensor'), may hold values from -6 to 6
- projector: bfloat16 [16384, 512], P('tensor'), may hold values from -0.046875 to 0.046875
- weight: float32 [1536, 16384], P('dp', 'tensor'), may hold values from -0.1 to 0.1
- first_moment: float32 [1536, 512], P('dp', 'tensor'), may hold values from -0.2 to 0.2
- second_moment: float32 [1536, 512], P('dp', 'tensor'), may hold values from 1e-05 to 0.001
Outputs:
- new_weight: float32 [1536, 16384], P('dp', 'tensor')
- new_first: float32 [1536, 512], P('dp', 'tensor')
- new_second: float32 [1536, 512], P('dp', 'tensor')
All inputs are finite; a program needn't handle non-finite values.
Results may differ from a plain program's by a relative error of at most 0.0016.
Values may be sent and summed in bfloat16 or wider, within the bound.
A program may use at most 64 MiB of HBM per device.

v0:
```python
import jax
import jax.numpy as jnp
from jax import lax
from jax.sharding import PartitionSpec as P


def body(grads, projector, weight, first_moment, second_moment):
    replicas = lax.axis_size("dp")
    splits = lax.axis_size("tensor")
    partial_value = jnp.dot(grads[0], projector, preferred_element_type=jnp.float32)
    shares = lax.psum_scatter(partial_value, "tensor", scatter_dimension=1, tiled=True)
    shares = lax.psum_scatter(shares, "dp", scatter_dimension=0, tiled=True)
    averaged = shares / replicas
    new_first = 0.9 * first_moment + 0.1 * averaged
    new_second = 0.999 * second_moment + 0.001 * averaged * averaged
    direction = (new_first / (jnp.sqrt(new_second) + 1e-08)).astype(jnp.bfloat16)
    update = lax.dot_general(
        lax.all_gather(direction, "tensor", axis=1, tiled=True),
        projector,
        (((1,), (1,)), ((), ())),
        preferred_element_type=jnp.float32,
    )
    total_sq = lax.psum(jnp.sum(update * update), ("dp", "tensor"))
    entries = float(update.shape[0] * update.shape[1] * replicas * splits)
    factor = jnp.minimum(1.0, 0.02 * jnp.sqrt(entries) / (jnp.sqrt(total_sq) + 1e-06))
    new_weight = weight - factor * update
    return (new_weight, new_first, new_second)


def solution(mesh):
    placed = (
        P("dp", None, "tensor"),
        P("tensor", None),
        P("dp", "tensor"),
        P("dp", "tensor"),
        P("dp", "tensor"),
    )
    return jax.shard_map(
        body,
        mesh=mesh,
        in_specs=placed,
        out_specs=(P("dp", "tensor"), P("dp", "tensor"), P("dp", "tensor")),
        check_vma=False,
    )
```

profile of v0, /device:TPU:1, one launch (start us, length us, event | category | flops | bytes accessed | tf_op | source)
XLA Modules:
  0.0 420.3 jit_solution(8280139943856687670)
XLA Ops:
  7.2 0.0 copy-start
  7.2 0.0 reduce-scatter.5.cloned.1.call-start
  7.2 1.8 copy-done
  9.1 4.7 %fusion = f32[1536,512]{0,1:T(8,128)} fusion(bf16[1024,512]{1,0:T(8,128)(2,1)} %param.6, bf16[1,1536,1024]{2,1,0:T(8,128)(2,1)S(1)} %copy-done), kind=kOutput, calls=%fused_computation | convolution fusion | flops 1610612736 | bytes 7340032 | tf_op jit(solution)/shard_map/dot_general | solution.py:10
  13.8 0.0 copy-start.2
  13.8 0.0 copy-start.3
  13.8 0.0 copy-start.1
  13.8 0.0 reduce-scatter.5.cloned.1.call-update
  13.8 0.0 reduce-scatter.7.cloned.1.call-start
  13.9 108.9 %reduce-scatter.5.cloned.1.call-done = f32[1536,32]{0,1:T(8,128)} async-done(((f32[1536,512]{0,1:T(8,128)}), f32[1536,32]{0,1:T(8,128)}) %reduce-scatter.5.cloned.1.call-update) | async-done | bytes 196624 | tf_op jit(solution)/shard_map/reduce_scatter | solution.py:11
  122.8 2.1 copy.8
  124.8 0.0 reduce-scatter.7.cloned.1.call-update
  124.9 133.9 %reduce-scatter.7.cloned.1.call-done = f32[48,32]{1,0:T(8,128)} async-done(((f32[1536,32]{1,0:T(8,128)}), f32[48,32]{1,0:T(8,128)}) %reduce-scatter.7.cloned.1.call-update) | async-done | bytes 6160
  258.8 0.8 copy.9
  259.6 0.0 copy-done.2
  259.6 0.0 copy-done.3
  259.6 0.6 divide_convert_fusion
  260.2 55.7 %all_gather.3 = bf16[48,512]{0,1:T(8,128)(2,1)S(1)} all-gather(bf16[48,32]{0,1:T(8,128)(2,1)S(1)} %get-tuple-element.3), channel_id=1, replica_groups=mesh['dp'=32,'tensor'=16] {'tensor'}, dimensions={1}, use_global_device_ids=true | all-gather | bytes 52224 | tf_op jit(solution)/shard_map/all_gather | solution.py:18
  315.9 2.3 multiply_reduce_fusion
  318.2 93.8 %psum.7 = f32[]{:T(128)} all-reduce(f32[]{:T(128)} %get-tuple-element.6), channel_id=1, replica_groups=mesh['dp'=32,'tensor'=16] {'dp','tensor'}, use_global_device_ids=true, to_apply=%region_3.0 | all-reduce | flops 1 | bytes 8 | tf_op jit(solution)/shard_map/psum | solution.py:23
  412.7 0.0 copy-done.1
  412.8 0.7 multiply_subtract_fusion
Async XLA Ops:
  7.2 1.9 copy-start
  7.2 115.6 %reduce-scatter.5.cloned.1.call-start = ((), (), s32[]{:S(2)}) async-start(), calls=%async_computation.2 | async-start | bytes 3342336 | tf_op jit(solution)/shard_map/reduce_scatter | solution.py:11
  13.8 245.8 %copy-start.2 = (f32[48,32]{0,1:T(8,128)S(1)}, f32[48,32]{0,1:T(8,128)}, u32[]{:S(2)}) copy-start(f32[48,32]{0,1:T(8,128)} %param.9) | copy-start | bytes 18436
  13.8 245.8 %copy-start.3 = (f32[48,32]{0,1:T(8,128)S(1)}, f32[48,32]{0,1:T(8,128)}, u32[]{:S(2)}) copy-start(f32[48,32]{0,1:T(8,128)} %param.8) | copy-start | bytes 18436
  13.8 399.0 %copy-start.1 = (f32[48,1024]{1,0:T(8,128)S(1)}, f32[48,1024]{1,0:T(8,128)}, u32[]{:S(2)}) copy-start(f32[48,1024]{1,0:T(8,128)} %param.7) | copy-start | bytes 589828
  13.8 245.0 %reduce-scatter.7.cloned.1.call-start = ((), (), s32[]{:S(2)}) async-start(), calls=%async_computation.3 | async-start | bytes 811008
Sparse Core Ops, SparseCore 0:
  13.9 108.7 reduce-scatter.4
  125.5 133.1 reduce-scatter.6
where the time goes:
time: 421 us; the launch traced here: 420 us
  waiting for transfers between devices  243 us (58%)
  blocking collectives  150 us (36%)
  between operations  14.8 us (4%)
  matrix products  6.99 us (2%)
  local copies, waits for them, and re-layouts  4.74 us (1%)
    unnamed x3, waiting for transfers between devices  134 us
    reduce_scatter x1, waiting for transfers between devices, body(): lax.psum_scatter(partial_value, 'tensor', scatter_dimension=1, tiled=True)  109 us
    psum x1, blocking collectives, body(): total_sq = lax.psum(jnp.sum(update * update), ('dp', 'tensor'))  93.8 us
    all_gather x1, blocking collectives, body(): lax.all_gather(direction, 'tensor', axis=1, tiled=True)  55.7 us
  transfers between devices with their start and end apart: 2, of which 2 were waited for; matrix products, arithmetic and copies ran while one was open for 0% of the time, Pallas kernels for 0%

commit v1 on v0

v1 whole, which is shorter than its diff:
```python
import jax
import jax.numpy as jnp
from jax import lax
from jax.experimental import pallas as pl
from jax.experimental.pallas import tpu as pltpu
from jax.sharding import PartitionSpec as P

MESH = pl.DeviceIdType.MESH
F32, BF16 = jnp.float32, jnp.bfloat16

NX, NY, NZ, NZLO = 4, 8, 8, 4
ROWS, HALF, COLS, TILE = 48, 24, 512, 128
DEPTH = 1024
CHUNK = NY * ROWS

CORE = [(0, 0, 0, 1)]
XS = [(d, 0, 0, 0) for d in range(1, NX)]
YS = [(0, d, 0, 0) for d in range(1, NY)]
ZS = [(0, 0, d, 0) for d in range(1, NZ)]
XC = [(d, 0, 0, k) for d in range(NX) for k in range(2) if (d, k) != (0, 0)]
HC = [(0, 0, h, k) for h in (0, 4) for k in range(2) if (h, k) != (0, 0)]
PARTNERS = list(dict.fromkeys(YS + ZS + HC + XC))


def kernel(
    grads, projector, weight, first, second,
    new_weight, new_first, new_second,
    gbuf, pbuf, ptbuf, wbuf, mom, acc, crecv, xsend, xrecv, ysend, yrecv, zown, zrecv,
    mrecv, pboth, dsend, dall, upd, ssend, sxrecv, syrecv, szrecv,
    lsem, core_s, core_r, x_s, x_r, y_s, y_r, z_s, z_r, m_s, m_r, d_s, d_r, p_s, p_r, s_s, s_r,
):
    dp, tensor = lax.axis_index("dp"), lax.axis_index("tensor")
    zlo, y = dp // NY, dp % NY
    x, zhi, core = tensor // 4, (tensor // 2) % 2, tensor % 2
    z = zhi * NZLO + zlo
    other = 1 - core
    quarter = zhi * 2 + core

    def at(delta):
        dx, dy, dz, dk = delta
        px, py, pz, pk = (x + dx) % NX, (y + dy) % NY, (z + dz) % NZ, (core + dk) % 2
        return ((pz % NZLO) * NY + py, px * 4 + (pz // NZLO) * 2 + pk)

    pending = []

    def send(src, dst, send_sem, recv_sem, delta):
        copy = pltpu.make_async_remote_copy(
            src_ref=src, dst_ref=dst, send_sem=send_sem, recv_sem=recv_sem,
            device_id=at(delta), device_id_type=MESH,
        )
        copy.start()
        pending.append(copy)
        return copy

    loads = [pltpu.make_async_copy(projector, pbuf, lsem.at[0])]
    for s in range(NZLO):
        chunk = (zlo + s + 1) % NZLO
        rows = pl.ds(pl.multiple_of(chunk * CHUNK, CHUNK), CHUNK)
        loads.append(pltpu.make_async_copy(grads.at[0, rows], gbuf.at[s], lsem.at[1 + s]))
    loads.append(pltpu.make_async_copy(first, mom.at[0], lsem.at[5]))
    loads.append(pltpu.make_async_copy(second, mom.at[1], lsem.at[6]))
    loads.append(pltpu.make_async_copy(weight, wbuf, lsem.at[7]))
    for load in loads:
        load.start()

    barrier = pltpu.get_barrier_semaphore()
    for delta in PARTNERS:
        pl.semaphore_signal(barrier, inc=1, device_id=at(delta), device_id_type=MESH)

    loads[0].wait()
    for s in range(NZLO):
        loads[1 + s].wait()

        @pl.loop(0, 2)
        def _(part):
            block = gbuf[s, pl.ds(pl.multiple_of(part * 192, 192), 192)]
            out = jnp.dot(block, pbuf[...], preferred_element_type=F32)
            acc[s, pl.ds(part * 4, 4)] = out.reshape(4, 2, HALF, COLS)

    ptbuf[...] = pbuf[...].T
    pl.semaphore_wait(barrier, len(PARTNERS))

    core_copies = [
        send(acc.at[s, :, other], crecv.at[s], core_s.at[s], core_r.at[s], CORE[0])
        for s in range(NZLO)
    ]
    loads[5].wait()
    loads[6].wait()
    m_copies = []
    for j, delta in enumerate(HC):
        target_half = (core + delta[3]) % 2
        rows = pl.ds(pl.multiple_of(target_half * HALF, 8), HALF)
        m_copies.append(send(mom.at[:, rows], mrecv.at[quarter], m_s.at[j], m_r.at[j], delta))
    mrecv[quarter] = mom[:, pl.ds(pl.multiple_of(core * HALF, 8), HALF)]

    x_copies = []
    for s in range(NZLO):
        core_copies[s].wait_recv()
        for j, delta in enumerate(XS):
            lanes = pl.ds(pl.multiple_of(((x + delta[0]) % NX) * TILE, TILE), TILE)
            tile = acc[s, :, core, :, lanes] + crecv[s, :, :, lanes]
            xsend[s, j] = tile.reshape(NY * HALF, TILE).astype(BF16)
            x_copies.append(send(xsend.at[s, j], xrecv.at[s, j], x_s.at[s, j], x_r.at[s, j], delta))

    y_copies = []
    for s in range(NZLO):
        for j in range(len(XS)):
            x_copies[s * len(XS) + j].wait_recv()
        lanes = pl.ds(pl.multiple_of(x * TILE, TILE), TILE)
        total = acc[s, :, core, :, lanes] + crecv[s, :, :, lanes]
        for j in range(len(XS)):
            total = total + xrecv[s, j].astype(F32).reshape(NY, HALF, TILE)
        ysend[s] = total
        for j, delta in enumerate(YS):
            y_copies.append(
                send(ysend.at[s, (y + delta[1]) % NY], yrecv.at[s, j], y_s.at[s, j], y_r.at[s, j], delta)
            )

    z_copies = {}
    for s in range(NZLO):
        for j in range(len(YS)):
            y_copies[s * len(YS) + j].wait_recv()
        total = ysend[s, y]
        for j in range(len(YS)):
            total = total + yrecv[s, j]
        zown[s] = total
        for d in (s + 1, s + 5):
            if d < NZ:
                z_copies[d] = send(zown.at[s], zrecv.at[d - 1], z_s.at[d - 1], z_r.at[d - 1], ZS[d - 1])

    for copy in m_copies:
        copy.wait_recv()
    m_first = jnp.concatenate([mrecv[q, 0] for q in range(4)], axis=1)
    m_second = jnp.concatenate([mrecv[q, 1] for q in range(4)], axis=1)
    total = zown[NZLO - 1]
    for d in range(1, NZ):
        z_copies[d].wait_recv()
        total = total + zrecv[d - 1]
    averaged = total * (1.0 / 32.0)

    def moments(old_first, old_second, mean):
        return 0.9 * old_first + 0.1 * mean, 0.999 * old_second + 0.001 * mean * mean

    f, v = moments(m_first, m_second, averaged)
    direction = f / (jnp.sqrt(v) + 1e-08)
    direction = jnp.concatenate([direction, jnp.zeros((8, TILE), F32)], axis=0).astype(BF16)
    dsend[...] = direction
    d_copies = []
    for j, delta in enumerate(XC):
        d_copies.append(send(dsend, dall.at[core, x], d_s.at[j], d_r.at[j], delta))
    pboth[core] = averaged
    p_copy = send(pboth.at[core], pboth.at[core], p_s, p_r, CORE[0])
    dall[core, x] = direction
    for copy in d_copies:
        copy.wait_recv()
    whole = jnp.concatenate(
        [jnp.concatenate([dall[k, t] for t in range(NX)], axis=1) for k in range(2)], axis=0
    )
    update = jnp.dot(whole, ptbuf[...], preferred_element_type=F32)
    update = jnp.concatenate([update[0:HALF], update[32:32 + HALF]], axis=0)
    upd[...] = update
    square = update * update
    folded = square[0:8]
    for r in range(1, ROWS // 8):
        folded = folded + square[8 * r:8 * r + 8]
    lanes_sum = folded[:, 0:TILE]
    for t in range(1, DEPTH // TILE):
        lanes_sum = lanes_sum + folded[:, t * TILE:(t + 1) * TILE]
    total = jnp.sum(lanes_sum, axis=0, keepdims=True)

    n = 0
    for r, (deltas, box) in enumerate(((XC, sxrecv), (YS, syrecv), (ZS, szrecv))):
        ssend[r] = total
        copies = []
        for j, delta in enumerate(deltas):
            copies.append(send(ssend.at[r], box.at[j], s_s.at[n], s_r.at[n], delta))
            n += 1
        if r == 0:
            p_copy.wait_recv()
            pieces = []
            for k in range(2):
                mean = pboth[k]
                piece = mean[:, 0:32]
                for q in range(1, 4):
                    piece = jnp.where(quarter == q, mean[:, 32 * q:32 * q + 32], piece)
                pieces.append(piece)
            f, v = moments(mom[0], mom[1], jnp.concatenate(pieces, axis=0))
            new_first[...] = f
            new_second[...] = v
            loads[7].wait()
        for j, copy in enumerate(copies):
            copy.wait_recv()
            total = total + box[j]

    total_sq = jnp.sum(total, axis=1, keepdims=True)
    entries = float(1536 * 16384)
    factor = jnp.minimum(1.0, 0.02 * entries**0.5 / (jnp.sqrt(total_sq) + 1e-06))
    new_weight[...] = wbuf[...] - factor * upd[...]
    for copy in pending:
        copy.wait_send()


def body(grads, projector, weight, first_moment, second_moment):
    sem = pltpu.SemaphoreType.DMA
    vm = pltpu.VMEM
    return pl.pallas_call(
        kernel,
        name="galore_step",
        out_shape=(
            jax.ShapeDtypeStruct((ROWS, DEPTH), F32),
            jax.ShapeDtypeStruct((ROWS, 32), F32),
            jax.ShapeDtypeStruct((ROWS, 32), F32),
        ),
        in_specs=[pl.BlockSpec(memory_space=pl.ANY)] * 5,
        out_specs=(pl.BlockSpec(memory_space=pltpu.VMEM),) * 3,
        scratch_shapes=[
            vm((NZLO, CHUNK, DEPTH), BF16),
            vm((DEPTH, COLS), BF16),
            vm((COLS, DEPTH), BF16),
            vm((ROWS, DEPTH), F32),
            vm((2, ROWS, 32), F32),
            vm((NZLO, NY, 2, HALF, COLS), F32),
            vm((NZLO, NY, HALF, COLS), F32),
            vm((NZLO, 3, NY * HALF, TILE), BF16),
            vm((NZLO, 3, NY * HALF, TILE), BF16),
            vm((NZLO, NY, HALF, TILE), F32),
            vm((NZLO, 7, HALF, TILE), F32),
            vm((NZLO, HALF, TILE), F32),
            vm((7, HALF, TILE), F32),
            vm((4, 2, HALF, 32), F32),
            vm((2, HALF, TILE), F32),
            vm((32, TILE), BF16),
            vm((2, NX, 32, TILE), BF16),
            vm((ROWS, DEPTH), F32),
            vm((3, 1, TILE), F32),
            vm((7, 1, TILE), F32),
            vm((7, 1, TILE), F32),
            vm((7, 1, TILE), F32),
            sem((8,)),
            sem((NZLO,)), sem((NZLO,)),
            sem((NZLO, 3)), sem((NZLO, 3)),
            sem((NZLO, 7)), sem((NZLO, 7)),
            sem((7,)), sem((7,)),
            sem((3,)), sem((3,)),
            sem((7,)), sem((7,)),
            sem, sem,
            sem((21,)), sem((21,)),
        ],
        compiler_params=pltpu.CompilerParams(
            collective_id=0, has_side_effects=True, vmem_limit_bytes=48 * 2**20
        ),
    )(grads, projector, weight, first_moment, second_moment)


def solution(mesh):
    placed = (
        P("dp", None, "tensor"),
        P("tensor", None),
        P("dp", "tensor"),
        P("dp", "tensor"),
        P("dp", "tensor"),
    )
    return jax.shard_map(
        body,
        mesh=mesh,
        in_specs=placed,
        out_specs=(P("dp", "tensor"), P("dp", "tensor"), P("dp", "tensor")),
        check_vma=False,
    )
```

time: 421 us -> 63.3 us (0.15)
  waiting for transfers between devices: 243 us -> 0 us
  blocking collectives: 150 us -> 0 us
  Pallas kernels: 0 us -> 54.6 us
  between operations: 14.8 us -> 0.64 us
  matrix products: 6.99 us -> 0 us
    unnamed x3 -> x0, waiting for transfers between devices: 134 us -> none
    reduce_scatter x1 -> x0, waiting for transfers between devices: 109 us -> none  [body(): lax.psum_scatter(partial_value, 'tensor', scatter_dimension=1, tiled=True)]
    psum x1 -> x0, blocking collectives: 93.8 us -> none  [body(): total_sq = lax.psum(jnp.sum(update * update), ('dp', 'tensor'))]
    all_gather x1 -> x0, blocking collectives: 55.7 us -> none  [body(): lax.all_gather(direction, 'tensor', axis=1, tiled=True)]
    pallas_call x0 -> x1, Pallas kernels: none -> 54.6 us  [body(): pl.pallas_call(kernel, name='galore_step', out_shape=(jax.ShapeDtypeStruc...]
    dot_general x2 -> x0, matrix products: 6.99 us -> none  [the longest x1 4.73 us: body(): jnp.dot(grads[0], projector, preferred_element_type=jnp.float32)]
  transfers between devices with their start and end apart: 2 -> 0, of which waited for: 2 -> 0; matrix products, arithmetic and copies ran while one was open for 0% -> 0% of each run, Pallas kernels for 0% -> 0%
where the time goes in v1:
time: 63.3 us; the launch traced here: 63 us
  Pallas kernels  54.6 us (86%)
  local copies, waits for them, and re-layouts  7.67 us (12%)
  between operations  0.64 us (1%)
    pallas_call x1, Pallas kernels, body(): pl.pallas_call(kernel, name='galore_step', out_shape=(jax.ShapeDtypeStruc...  54.6 us
    unnamed x9, local copies, waits for them, and re-layouts  6.31 us
    pallas_call x2, local copies, waits for them, and re-layouts, body(): pl.pallas_call(kernel, name='galore_step', out_shape=(jax.ShapeDtypeStruc...  1.36 us

profile of v1, /device:TPU:1, one launch (start us, length us, event | category | flops | bytes accessed | tf_op | source)
XLA Modules:
  0.0 63.0 jit_solution(6528337661825536707)
XLA Ops:
  0.6 0.8 %copy.8.first = f32[48,32]{1,0:T(8,128)S(1)} copy(f32[48,32]{0,1:T(8,128)} %param.8) | data formatting | bytes 12288 | tf_op args[3]
  1.4 0.8 %copy.9.second = f32[48,32]{1,0:T(8,128)S(1)} copy(f32[48,32]{0,1:T(8,128)} %param.9) | data formatting | bytes 12288 | tf_op args[4]
  2.2 0.0 copy-start
  2.2 1.9 %copy-done = bf16[1,1536,1024]{2,1,0:T(8,128)(2,1)S(1)} copy-done((bf16[1,1536,1024]{2,1,0:T(8,128)(2,1)S(1)}, bf16[1,1536,1024]{2,1,0:T(8,128)(2,1)}, u32[]{:S(2)}) %copy-start) | copy-done | bytes 3145752
  4.1 0.0 copy-start.1
  4.1 1.2 %copy-done.1 = bf16[1024,512]{1,0:T(8,128)(2,1)S(1)} copy-done((bf16[1024,512]{1,0:T(8,128)(2,1)S(1)}, bf16[1024,512]{1,0:T(8,128)(2,1)}, u32[]{:S(2)}) %copy-start.1) | copy-done | bytes 1048600
  5.3 0.0 copy-start.2
  5.3 0.9 %copy-done.2 = f32[48,1024]{1,0:T(8,128)S(1)} copy-done((f32[48,1024]{1,0:T(8,128)S(1)}, f32[48,1024]{1,0:T(8,128)}, u32[]{:S(2)}) %copy-start.2) | copy-done | bytes 196632
  6.3 54.6 %galore_step.1 = (f32[48,1024]{1,0:T(8,128)S(1)}, f32[48,32]{1,0:T(8,128)S(1)}, f32[48,32]{1,0:T(8,128)S(1)}) custom-call(bf16[1,1536,1024]{2,1,0:T(8,128)(2,1)S(1)} %copy-done, bf16[1024,512]{1,0:T(8,128)(2,1)S(1)} %copy-done.1, f32[48,1024]{1,0:T(8,128)S(1)} %copy-done.2, f32[48,32]{1,0:T(8,128)S(1)} %copy.8.first, f32[48,32]{1,0:T(8,128)S(1)} %copy.9.second), custom_call_target="tpu_custom_call" | custom-call | tf_op jit(solution)/shard_map/galore_step/pallas_call | solution.py:206
  60.9 0.7 %copy.10 = f32[48,32]{0,1:T(8,128)} copy(f32[48,32]{1,0:T(8,128)S(1)} %get-tuple-element.4) | data formatting | bytes 12288 | tf_op jit(solution)/shard_map/galore_step/pallas_call | solution.py:206
  61.6 0.7 %copy.11 = f32[48,32]{0,1:T(8,128)} copy(f32[48,32]{1,0:T(8,128)S(1)} %get-tuple-element.5) | data formatting | bytes 12288 | tf_op jit(solution)/shard_map/galore_step/pallas_call | solution.py:206
  62.3 0.7 %copy.13 = f32[48,1024]{1,0:T(8,128)} copy(f32[48,1024]{1,0:T(8,128)S(1)} %get-tuple-element.9) | data formatting | bytes 393216
Async XLA Ops:
  2.2 1.9 %copy-start = (bf16[1,1536,1024]{2,1,0:T(8,128)(2,1)S(1)}, bf16[1,1536,1024]{2,1,0:T(8,128)(2,1)}, u32[]{:S(2)}) copy-start(bf16[1,1536,1024]{2,1,0:T(8,128)(2,1)} %grads.1) | copy-start | bytes 9437188
  4.1 1.2 %copy-start.1 = (bf16[1024,512]{1,0:T(8,128)(2,1)S(1)}, bf16[1024,512]{1,0:T(8,128)(2,1)}, u32[]{:S(2)}) copy-start(bf16[1024,512]{1,0:T(8,128)(2,1)} %projector.1) | copy-start | bytes 3145732
  5.3 0.9 %copy-start.2 = (f32[48,1024]{1,0:T(8,128)S(1)}, f32[48,1024]{1,0:T(8,128)}, u32[]{:S(2)}) copy-start(f32[48,1024]{1,0:T(8,128)} %weight.1) | copy-start | bytes 589828

commit v2 on v1

--- a/solution.py
+++ b/solution.py
@@ -22,10 +22,17 @@
 PARTNERS = list(dict.fromkeys(YS + ZS + HC + XC))
 
 
+def flip(block):
+    rows, cols = block.shape
+    wide = jnp.concatenate([block, jnp.zeros((rows, 128 - cols), F32)], axis=1)
+    square = jnp.concatenate([wide, jnp.zeros((128 - rows, 128), F32)], axis=0)
+    return square.T[:cols, :rows]
+
+
 def kernel(
-    grads, projector, weight, first, second,
-    new_weight, new_first, new_second,
-    gbuf, pbuf, ptbuf, wbuf, mom, acc, crecv, xsend, xrecv, ysend, yrecv, zown, zrecv,
+    grads, projector, first, second,
+    step, mean_t,
+    gbuf, pbuf, ptbuf, mom_t, mom, acc, crecv, xsend, xrecv, ysend, yrecv, zown, zrecv,
     mrecv, pboth, dsend, dall, upd, ssend, sxrecv, syrecv, szrecv,
     lsem, core_s, core_r, x_s, x_r, y_s, y_r, z_s, z_r, m_s, m_r, d_s, d_r, p_s, p_r, s_s, s_r,
 ):
@@ -57,9 +64,8 @@
         chunk = (zlo + s + 1) % NZLO
         rows = pl.ds(pl.multiple_of(chunk * CHUNK, CHUNK), CHUNK)
         loads.append(pltpu.make_async_copy(grads.at[0, rows], gbuf.at[s], lsem.at[1 + s]))
-    loads.append(pltpu.make_async_copy(first, mom.at[0], lsem.at[5]))
-    loads.append(pltpu.make_async_copy(second, mom.at[1], lsem.at[6]))
-    loads.append(pltpu.make_async_copy(weight, wbuf, lsem.at[7]))
+    loads.append(pltpu.make_async_copy(first, mom_t.at[0], lsem.at[5]))
+    loads.append(pltpu.make_async_copy(second, mom_t.at[1], lsem.at[6]))
     for load in loads:
         load.start()
 
@@ -67,15 +73,15 @@
     for delta in PARTNERS:
         pl.semaphore_signal(barrier, inc=1, device_id=at(delta), device_id_type=MESH)
 
+    loads[5].wait()
+    loads[6].wait()
+    mom[0] = flip(mom_t[0])
+    mom[1] = flip(mom_t[1])
     loads[0].wait()
     for s in range(NZLO):
         loads[1 + s].wait()
-
-        @pl.loop(0, 2)
-        def _(part):
-            block = gbuf[s, pl.ds(pl.multiple_of(part * 192, 192), 192)]
-            out = jnp.dot(block, pbuf[...], preferred_element_type=F32)
-            acc[s, pl.ds(part * 4, 4)] = out.reshape(4, 2, HALF, COLS)
+        out = jnp.dot(gbuf[s], pbuf[...], preferred_element_type=F32)
+        acc[s] = out.reshape(NY, 2, HALF, COLS)
 
     ptbuf[...] = pbuf[...].T
     pl.semaphore_wait(barrier, len(PARTNERS))
@@ -84,8 +90,6 @@
         send(acc.at[s, :, other], crecv.at[s], core_s.at[s], core_r.at[s], CORE[0])
         for s in range(NZLO)
     ]
-    loads[5].wait()
-    loads[6].wait()
     m_copies = []
     for j, delta in enumerate(HC):
         target_half = (core + delta[3]) % 2
@@ -184,10 +188,7 @@
                 for q in range(1, 4):
                     piece = jnp.where(quarter == q, mean[:, 32 * q:32 * q + 32], piece)
                 pieces.append(piece)
-            f, v = moments(mom[0], mom[1], jnp.concatenate(pieces, axis=0))
-            new_first[...] = f
-            new_second[...] = v
-            loads[7].wait()
+            mean_t[...] = flip(jnp.concatenate(pieces, axis=0))
         for j, copy in enumerate(copies):
             copy.wait_recv()
             total = total + box[j]
@@ -195,7 +196,7 @@
     total_sq = jnp.sum(total, axis=1, keepdims=True)
     entries = float(1536 * 16384)
     factor = jnp.minimum(1.0, 0.02 * entries**0.5 / (jnp.sqrt(total_sq) + 1e-06))
-    new_weight[...] = wbuf[...] - factor * upd[...]
+    step[...] = factor * upd[...]
     for copy in pending:
         copy.wait_send()
 
@@ -203,21 +204,21 @@
 def body(grads, projector, weight, first_moment, second_moment):
     sem = pltpu.SemaphoreType.DMA
     vm = pltpu.VMEM
-    return pl.pallas_call(
+    operands = (grads, projector, first_moment.T, second_moment.T)
+    step, mean_t = pl.pallas_call(
         kernel,
         name="galore_step",
         out_shape=(
             jax.ShapeDtypeStruct((ROWS, DEPTH), F32),
-            jax.ShapeDtypeStruct((ROWS, 32), F32),
-            jax.ShapeDtypeStruct((ROWS, 32), F32),
+            jax.ShapeDtypeStruct((32, ROWS), F32),
         ),
-        in_specs=[pl.BlockSpec(memory_space=pl.ANY)] * 5,
-        out_specs=(pl.BlockSpec(memory_space=pltpu.VMEM),) * 3,
+        in_specs=[pl.BlockSpec(memory_space=pltpu.HBM)] * 4,
+        out_specs=(pl.BlockSpec(memory_space=pltpu.VMEM),) * 2,
         scratch_shapes=[
             vm((NZLO, CHUNK, DEPTH), BF16),
             vm((DEPTH, COLS), BF16),
             vm((COLS, DEPTH), BF16),
-            vm((ROWS, DEPTH), F32),
+            vm((2, 32, ROWS), F32),
             vm((2, ROWS, 32), F32),
             vm((NZLO, NY, 2, HALF, COLS), F32),
             vm((NZLO, NY, HALF, COLS), F32),
@@ -236,7 +237,7 @@
             vm((7, 1, TILE), F32),
             vm((7, 1, TILE), F32),
             vm((7, 1, TILE), F32),
-            sem((8,)),
+            sem((7,)),
             sem((NZLO,)), sem((NZLO,)),
             sem((NZLO, 3)), sem((NZLO, 3)),
             sem((NZLO, 7)), sem((NZLO, 7)),
@@ -249,7 +250,11 @@
         compiler_params=pltpu.CompilerParams(
             collective_id=0, has_side_effects=True, vmem_limit_bytes=48 * 2**20
         ),
-    )(grads, projector, weight, first_moment, second_moment)
+    )(*(pltpu.with_memory_space_constraint(a, pltpu.HBM) for a in operands))
+    mean = mean_t.T
+    new_first = 0.9 * first_moment + 0.1 * mean
+    new_second = 0.999 * second_moment + 0.001 * mean * mean
+    return weight - step, new_first, new_second
 
 
 def solution(mesh):

time: 63.3 us -> 56.8 us (0.90)
  local copies, waits for them, and re-layouts: 7.67 us -> 0.01 us
  other arithmetic: 0 us -> 1.32 us
    unnamed x9 -> x6, local copies, waits for them, and re-layouts: 6.31 us -> 0.01 us
    pallas_call x2 -> x0, local copies, waits for them, and re-layouts: 1.36 us -> none  [body(): pl.pallas_call(kernel, name='galore_step', out_shape=(jax.ShapeDtypeStruc...]
    sub x0 -> x1, other arithmetic: none -> 0.7 us  [body(): return (weight - step, new_first, new_second)]
where the time goes in v2:
time: 56.8 us; the launch traced here: 56.3 us
  Pallas kernels  54.3 us (96%)
  other arithmetic  1.32 us (2%)
  between operations  0.67 us (1%)
    pallas_call x1, Pallas kernels, body(): pl.pallas_call(kernel, name='galore_step', out_shape=(jax.ShapeDtypeStruc...  54.3 us

profile of v2, /device:TPU:1, one launch (start us, length us, event | category | flops | bytes accessed | tf_op | source)
XLA Modules:
  0.0 56.3 jit_solution(4129631790933227122)
XLA Ops:
  0.6 0.0 copy-start.2
  0.6 0.0 copy-start.1
  0.7 0.0 copy-start
  0.7 54.3 %galore_step.1 = (f32[48,1024]{1,0:T(8,128)S(1)}, f32[32,48]{1,0:T(8,128)S(1)}) custom-call(bf16[1,1536,1024]{2,1,0:T(8,128)(2,1)} %grads.1, bf16[1024,512]{1,0:T(8,128)(2,1)} %projector.1, f32[32,48]{1,0:T(8,128)} %bitcast.7, f32[32,48]{1,0:T(8,128)} %bitcast.8), custom_call_target="tpu_custom_call" | custom-call | tf_op jit(solution)/shard_map/galore_step/pallas_call | solution.py:208
  55.0 0.0 copy-done
  55.0 0.7 %sub.3 = f32[48,1024]{1,0:T(8,128)} subtract(f32[48,1024]{1,0:T(8,128)S(1)} %copy-done, f32[48,1024]{1,0:T(8,128)S(1)} %get-tuple-element.5) | non-fusion elementwise | flops 49152 | bytes 589824 | tf_op jit(solution)/shard_map/sub | solution.py:257
  55.7 0.0 copy-done.2
  55.7 0.0 copy-done.1
  55.7 0.6 %fusion = (f32[48,32]{0,1:T(8,128)}, f32[48,32]{0,1:T(8,128)}) fusion(f32[32,48]{1,0:T(8,128)S(1)} %get-tuple-element.6, f32[48,32]{0,1:T(8,128)S(1)} %copy-done.2, f32[48,32]{0,1:T(8,128)S(1)} %copy-done.1), kind=kLoop, calls=%fused_computation.1 | loop fusion | flops 10752 | bytes 30720 | tf_op jit(solution)/shard_map/add | solution.py:256
Async XLA Ops:
  0.6 55.1 %copy-start.2 = (f32[48,32]{0,1:T(8,128)S(1)}, f32[48,32]{0,1:T(8,128)}, u32[]{:S(2)}) copy-start(f32[48,32]{0,1:T(8,128)} %param.9) | copy-start | bytes 18436
  0.6 55.1 %copy-start.1 = (f32[48,32]{0,1:T(8,128)S(1)}, f32[48,32]{0,1:T(8,128)}, u32[]{:S(2)}) copy-start(f32[48,32]{0,1:T(8,128)} %param.8) | copy-start | bytes 18436
  0.7 54.4 %copy-start = (f32[48,1024]{1,0:T(8,128)S(1)}, f32[48,1024]{1,0:T(8,128)}, u32[]{:S(2)}) copy-start(f32[48,1024]{1,0:T(8,128)} %param.7) | copy-start | bytes 589828

commit v3 on v2

--- a/solution.py
+++ b/solution.py
@@ -12,6 +12,8 @@
 ROWS, HALF, COLS, TILE = 48, 24, 512, 128
 DEPTH = 1024
 CHUNK = NY * ROWS
+GREET = 1
+STRIPE = 64
 
 CORE = [(0, 0, 0, 1)]
 XS = [(d, 0, 0, 0) for d in range(1, NX)]
@@ -33,8 +35,10 @@
     grads, projector, first, second,
     step, mean_t,
     gbuf, pbuf, ptbuf, mom_t, mom, acc, crecv, xsend, xrecv, ysend, yrecv, zown, zrecv,
-    mrecv, pboth, dsend, dall, upd, ssend, sxrecv, syrecv, szrecv,
+    yfsend, yfrecv, xfsum, xfrecv, gram, gcsend, gcrecv, gsum, gxsend, gxrecv, gfull,
+    mrecv, pboth, dsend, dall, upd, ssend, syrecv, szrecv,
     lsem, core_s, core_r, x_s, x_r, y_s, y_r, z_s, z_r, m_s, m_r, d_s, d_r, p_s, p_r, s_s, s_r,
+    yf_s, yf_r, xf_s, xf_r, gc_s, gc_r, gx_s, gx_r, ga_s, ga_r, gb_s, gb_r,
 ):
     dp, tensor = lax.axis_index("dp"), lax.axis_index("tensor")
     zlo, y = dp // NY, dp % NY
@@ -78,18 +82,24 @@
     mom[0] = flip(mom_t[0])
     mom[1] = flip(mom_t[1])
     loads[0].wait()
+    core_copies = []
+
+    def core_send(s):
+        core_copies.append(
+            send(acc.at[s, :, other], crecv.at[s], core_s.at[s], core_r.at[s], CORE[0])
+        )
+
     for s in range(NZLO):
         loads[1 + s].wait()
         out = jnp.dot(gbuf[s], pbuf[...], preferred_element_type=F32)
         acc[s] = out.reshape(NY, 2, HALF, COLS)
-
-    ptbuf[...] = pbuf[...].T
-    pl.semaphore_wait(barrier, len(PARTNERS))
-
-    core_copies = [
-        send(acc.at[s, :, other], crecv.at[s], core_s.at[s], core_r.at[s], CORE[0])
-        for s in range(NZLO)
-    ]
+        if s == GREET:
+            pl.semaphore_wait(barrier, len(PARTNERS))
+            for t in range(s):
+                core_send(t)
+        if s >= GREET:
+            core_send(s)
+
     m_copies = []
     for j, delta in enumerate(HC):
         target_half = (core + delta[3]) % 2
@@ -97,40 +107,101 @@
         m_copies.append(send(mom.at[:, rows], mrecv.at[quarter], m_s.at[j], m_r.at[j], delta))
     mrecv[quarter] = mom[:, pl.ds(pl.multiple_of(core * HALF, 8), HALF)]
 
-    x_copies = []
-    for s in range(NZLO):
+    def stacked(block):
+        return jnp.concatenate([block[:, t * TILE:(t + 1) * TILE] for t in range(NX)], axis=0)
+
+    core_copies[0].wait_recv()
+    yf_copies = []
+    for j, delta in enumerate(YS):
+        there = (y + delta[1]) % NY
+        yfsend[j] = stacked(acc[0, there, core] + crecv[0, there]).astype(BF16)
+        yf_copies.append(send(yfsend.at[j], yfrecv.at[j], yf_s.at[j], yf_r.at[j], delta))
+
+    x_copies = {}
+    for s in range(1, NZLO):
         core_copies[s].wait_recv()
         for j, delta in enumerate(XS):
             lanes = pl.ds(pl.multiple_of(((x + delta[0]) % NX) * TILE, TILE), TILE)
             tile = acc[s, :, core, :, lanes] + crecv[s, :, :, lanes]
-            xsend[s, j] = tile.reshape(NY * HALF, TILE).astype(BF16)
-            x_copies.append(send(xsend.at[s, j], xrecv.at[s, j], x_s.at[s, j], x_r.at[s, j], delta))
-
-    y_copies = []
-    for s in range(NZLO):
+            xsend[s - 1, j] = tile.reshape(NY * HALF, TILE).astype(BF16)
+            x_copies[s, j] = send(
+                xsend.at[s - 1, j], xrecv.at[s - 1, j], x_s.at[s - 1, j], x_r.at[s - 1, j], delta
+            )
+
+    gram[...] = lax.dot_general(
+        pbuf[...], pbuf[...], (((0,), (0,)), ((), ())), preferred_element_type=F32
+    ).reshape(2, COLS // 2, COLS)
+    gcsend[...] = gram[other].astype(BF16)
+    gc_copy = send(gcsend, gcrecv, gc_s, gc_r, CORE[0])
+    ptbuf[...] = pbuf[...].T
+
+    y_copies = {}
+    xf_copies = []
+
+    def along_y(s):
         for j in range(len(XS)):
-            x_copies[s * len(XS) + j].wait_recv()
+            x_copies[s, j].wait_recv()
         lanes = pl.ds(pl.multiple_of(x * TILE, TILE), TILE)
         total = acc[s, :, core, :, lanes] + crecv[s, :, :, lanes]
         for j in range(len(XS)):
-            total = total + xrecv[s, j].astype(F32).reshape(NY, HALF, TILE)
-        ysend[s] = total
+            total = total + xrecv[s - 1, j].astype(F32).reshape(NY, HALF, TILE)
+        ysend[s - 1] = total
         for j, delta in enumerate(YS):
-            y_copies.append(
-                send(ysend.at[s, (y + delta[1]) % NY], yrecv.at[s, j], y_s.at[s, j], y_r.at[s, j], delta)
+            y_copies[s, j] = send(
+                ysend.at[s - 1, (y + delta[1]) % NY], yrecv.at[s - 1, j],
+                y_s.at[s - 1, j], y_r.at[s - 1, j], delta,
             )
 
+    def along_x_after():
+        total = stacked(acc[0, y, core] + crecv[0, y])
+        for j in range(len(YS)):
+            yf_copies[j].wait_recv()
+            total = total + yfrecv[j].astype(F32)
+        xfsum[...] = total.reshape(NX, HALF, TILE)
+        for j, delta in enumerate(XS):
+            xf_copies.append(
+                send(xfsum.at[(x + delta[0]) % NX], xfrecv.at[j], xf_s.at[j], xf_r.at[j], delta)
+            )
+
+    along_y(1)
+    along_y(2)
+    along_x_after()
+    along_y(3)
+
+    gc_copy.wait_recv()
+    gsum[...] = (gram[core] + gcrecv[...].astype(F32)).reshape(NX, STRIPE, COLS)
+    gx_copies = []
+    for j, delta in enumerate(XS):
+        gxsend[j] = gsum[(x + delta[0]) % NX].astype(BF16)
+        gx_copies.append(send(gxsend.at[j], gxrecv.at[j], gx_s.at[j], gx_r.at[j], delta))
+
     z_copies = {}
-    for s in range(NZLO):
-        for j in range(len(YS)):
-            y_copies[s * len(YS) + j].wait_recv()
-        total = ysend[s, y]
-        for j in range(len(YS)):
-            total = total + yrecv[s, j]
+    for s in (1, 0, 2, 3):
+        if s == 0:
+            total = xfsum[x]
+            for j in range(len(XS)):
+                xf_copies[j].wait_recv()
+                total = total + xfrecv[j]
+        else:
+            total = ysend[s - 1, y]
+            for j in range(len(YS)):
+                y_copies[s, j].wait_recv()
+                total = total + yrecv[s - 1, j]
         zown[s] = total
         for d in (s + 1, s + 5):
             if d < NZ:
                 z_copies[d] = send(zown.at[s], zrecv.at[d - 1], z_s.at[d - 1], z_r.at[d - 1], ZS[d - 1])
+
+    stripe = gsum[x]
+    for j in range(len(XS)):
+        gx_copies[j].wait_recv()
+        stripe = stripe + gxrecv[j].astype(F32)
+    gfull[core, x] = stripe.astype(BF16)
+    ga_copies = []
+    for j, delta in enumerate(XS):
+        ga_copies.append(
+            send(gfull.at[core, x], gfull.at[core, x], ga_s.at[j], ga_r.at[j], delta)
+        )
 
     for copy in m_copies:
         copy.wait_recv()
@@ -155,31 +226,35 @@
     pboth[core] = averaged
     p_copy = send(pboth.at[core], pboth.at[core], p_s, p_r, CORE[0])
     dall[core, x] = direction
+    for copy in ga_copies:
+        copy.wait_recv()
+    gb_copy = send(gfull.at[core], gfull.at[core], gb_s, gb_r, CORE[0])
     for copy in d_copies:
         copy.wait_recv()
     whole = jnp.concatenate(
         [jnp.concatenate([dall[k, t] for t in range(NX)], axis=1) for k in range(2)], axis=0
     )
-    update = jnp.dot(whole, ptbuf[...], preferred_element_type=F32)
-    update = jnp.concatenate([update[0:HALF], update[32:32 + HALF]], axis=0)
-    upd[...] = update
-    square = update * update
+    gb_copy.wait_recv()
+    square = jnp.dot(whole, gfull[...].reshape(COLS, COLS), preferred_element_type=F32)
+    square = square * whole.astype(F32)
     folded = square[0:8]
-    for r in range(1, ROWS // 8):
+    for r in range(1, 8):
         folded = folded + square[8 * r:8 * r + 8]
     lanes_sum = folded[:, 0:TILE]
-    for t in range(1, DEPTH // TILE):
+    for t in range(1, NX):
         lanes_sum = lanes_sum + folded[:, t * TILE:(t + 1) * TILE]
     total = jnp.sum(lanes_sum, axis=0, keepdims=True)
 
     n = 0
-    for r, (deltas, box) in enumerate(((XC, sxrecv), (YS, syrecv), (ZS, szrecv))):
+    for r, (deltas, box) in enumerate(((YS, syrecv), (ZS, szrecv))):
         ssend[r] = total
         copies = []
         for j, delta in enumerate(deltas):
             copies.append(send(ssend.at[r], box.at[j], s_s.at[n], s_r.at[n], delta))
             n += 1
         if r == 0:
+            update = jnp.dot(whole, ptbuf[...], preferred_element_type=F32)
+            upd[...] = jnp.concatenate([update[0:HALF], update[32:32 + HALF]], axis=0)
             p_copy.wait_recv()
             pieces = []
             for k in range(2):
@@ -222,30 +297,46 @@
             vm((2, ROWS, 32), F32),
             vm((NZLO, NY, 2, HALF, COLS), F32),
             vm((NZLO, NY, HALF, COLS), F32),
-            vm((NZLO, 3, NY * HALF, TILE), BF16),
-            vm((NZLO, 3, NY * HALF, TILE), BF16),
-            vm((NZLO, NY, HALF, TILE), F32),
-            vm((NZLO, 7, HALF, TILE), F32),
+            vm((3, 3, NY * HALF, TILE), BF16),
+            vm((3, 3, NY * HALF, TILE), BF16),
+            vm((3, NY, HALF, TILE), F32),
+            vm((3, 7, HALF, TILE), F32),
             vm((NZLO, HALF, TILE), F32),
             vm((7, HALF, TILE), F32),
+            vm((7, NX * HALF, TILE), BF16),
+            vm((7, NX * HALF, TILE), BF16),
+            vm((NX, HALF, TILE), F32),
+            vm((3, HALF, TILE), F32),
+            vm((2, COLS // 2, COLS), F32),
+            vm((COLS // 2, COLS), BF16),
+            vm((COLS // 2, COLS), BF16),
+            vm((NX, STRIPE, COLS), F32),
+            vm((3, STRIPE, COLS), BF16),
+            vm((3, STRIPE, COLS), BF16),
+            vm((2, NX, STRIPE, COLS), BF16),
             vm((4, 2, HALF, 32), F32),
             vm((2, HALF, TILE), F32),
             vm((32, TILE), BF16),
             vm((2, NX, 32, TILE), BF16),
             vm((ROWS, DEPTH), F32),
-            vm((3, 1, TILE), F32),
-            vm((7, 1, TILE), F32),
+            vm((2, 1, TILE), F32),
             vm((7, 1, TILE), F32),
             vm((7, 1, TILE), F32),
             sem((7,)),
             sem((NZLO,)), sem((NZLO,)),
-            sem((NZLO, 3)), sem((NZLO, 3)),
-            sem((NZLO, 7)), sem((NZLO, 7)),
+            sem((3, 3)), sem((3, 3)),
+            sem((3, 7)), sem((3, 7)),
             sem((7,)), sem((7,)),
             sem((3,)), sem((3,)),
             sem((7,)), sem((7,)),
             sem, sem,
-            sem((21,)), sem((21,)),
+            sem((14,)), sem((14,)),
+            sem((7,)), sem((7,)),
+            sem((3,)), sem((3,)),
+            sem, sem,
+            sem((3,)), sem((3,)),
+            sem((3,)), sem((3,)),
+            sem, sem,
         ],
         compiler_params=pltpu.CompilerParams(
             collective_id=0, has_side_effects=True, vmem_limit_bytes=48 * 2**20

time: 56.8 us -> 51.6 us (0.908)
  Pallas kernels: 54.3 us -> 49.4 us
    pallas_call x1, Pallas kernels: 54.3 us -> 49.4 us  [body(): pl.pallas_call(kernel, name='galore_step', out_shape=(jax.ShapeDtypeStruc...]
where the time goes in v3:
time: 51.6 us; the launch traced here: 51.4 us
  Pallas kernels  49.4 us (96%)
  other arithmetic  1.32 us (3%)
  between operations  0.67 us (1%)
    pallas_call x1, Pallas kernels, body(): pl.pallas_call(kernel, name='galore_step', out_shape=(jax.ShapeDtypeStruc...  49.4 us

profile of v3, /device:TPU:1, one launch (start us, length us, event | category | flops | bytes accessed | tf_op | source)
XLA Modules:
  0.0 51.4 jit_solution(8556811294723596439)
XLA Ops:
  0.6 0.0 copy-start.2
  0.6 0.0 copy-start.1
  0.7 0.0 copy-start
  0.7 49.4 %galore_step.1 = (f32[48,1024]{1,0:T(8,128)S(1)}, f32[32,48]{1,0:T(8,128)S(1)}) custom-call(bf16[1,1536,1024]{2,1,0:T(8,128)(2,1)} %grads.1, bf16[1024,512]{1,0:T(8,128)(2,1)} %projector.1, f32[32,48]{1,0:T(8,128)} %bitcast.7, f32[32,48]{1,0:T(8,128)} %bitcast.8), custom_call_target="tpu_custom_call" | custom-call | tf_op jit(solution)/shard_map/galore_step/pallas_call | solution.py:283
  50.1 0.0 copy-done
  50.1 0.7 %sub.3 = f32[48,1024]{1,0:T(8,128)} subtract(f32[48,1024]{1,0:T(8,128)S(1)} %copy-done, f32[48,1024]{1,0:T(8,128)S(1)} %get-tuple-element.5) | non-fusion elementwise | flops 49152 | bytes 589824 | tf_op jit(solution)/shard_map/sub | solution.py:348
  50.8 0.0 copy-done.2
  50.8 0.0 copy-done.1
  50.8 0.6 %fusion = (f32[48,32]{0,1:T(8,128)}, f32[48,32]{0,1:T(8,128)}) fusion(f32[32,48]{1,0:T(8,128)S(1)} %get-tuple-element.6, f32[48,32]{0,1:T(8,128)S(1)} %copy-done.2, f32[48,32]{0,1:T(8,128)S(1)} %copy-done.1), kind=kLoop, calls=%fused_computation.1 | loop fusion | flops 10752 | bytes 30720 | tf_op jit(solution)/shard_map/add | solution.py:347
Async XLA Ops:
  0.6 50.2 %copy-start.2 = (f32[48,32]{0,1:T(8,128)S(1)}, f32[48,32]{0,1:T(8,128)}, u32[]{:S(2)}) copy-start(f32[48,32]{0,1:T(8,128)} %param.9) | copy-start | bytes 18436
  0.6 50.2 %copy-start.1 = (f32[48,32]{0,1:T(8,128)S(1)}, f32[48,32]{0,1:T(8,128)}, u32[]{:S(2)}) copy-start(f32[48,32]{0,1:T(8,128)} %param.8) | copy-start | bytes 18436
  0.7 49.5 %copy-start = (f32[48,1024]{1,0:T(8,128)S(1)}, f32[48,1024]{1,0:T(8,128)}, u32[]{:S(2)}) copy-start(f32[48,1024]{1,0:T(8,128)} %param.7) | copy-start | bytes 589828

commit v4 on v3

v4 whole, which is shorter than its diff:
```python
import jax
import jax.numpy as jnp
from jax import lax
from jax.experimental import pallas as pl
from jax.experimental.pallas import tpu as pltpu
from jax.sharding import PartitionSpec as P

MESH = pl.DeviceIdType.MESH
F32, BF16 = jnp.float32, jnp.bfloat16

NX, NY, NZ, NZLO = 4, 8, 8, 4
ROWS, HALF, COLS, TILE = 48, 24, 512, 128
DEPTH = 1024
CHUNK = NY * ROWS

G_CORE, G_X, G_XL, G_Y, G_Z, G_M, G_D, G_P, G_SY, G_SZ = 0, 4, 6, 8, 11, 12, 13, 14, 15, 16
G_YF, G_XF, G_GC, G_GX, G_GA, G_GB, GROUPS = 17, 18, 19, 20, 21, 22, 23
GREET = 1
YF = 1
XF = (0, 2)
OWNER = (0, 1, 3, 2)
LAST = NZLO - 1
PARTS = ((4, 3, 5, 6), (2, 1, 7, 0))
STRIPE = 64
PADDED = 32

CORE = [(0, 0, 0, 1)]


def hops(delta):
    return sum(min(d, n - d) for d, n in zip(delta, (NX, NY, NZ, 2)))


def farthest_first(deltas):
    return sorted(deltas, key=hops, reverse=True)


XS = farthest_first([(d, 0, 0, 0) for d in range(1, NX)])
YS = farthest_first([(0, d, 0, 0) for d in range(1, NY)])
ZS = farthest_first([(0, 0, d, 0) for d in range(1, NZ)])
XC = farthest_first([(d, 0, 0, k) for d in range(NX) for k in range(2) if (d, k) != (0, 0)])
HC = farthest_first([(0, 0, h, k) for h in (0, 4) for k in range(2) if (h, k) != (0, 0)])
PARTNERS = farthest_first(dict.fromkeys(YS + ZS + HC + XC))


def flip(block):
    rows, cols = block.shape
    wide = jnp.concatenate([block, jnp.zeros((rows, 128 - cols), F32)], axis=1)
    square = jnp.concatenate([wide, jnp.zeros((128 - rows, 128), F32)], axis=0)
    return square.T[:cols, :rows]


def kernel(
    grads, projector, first, second,
    step, mean_t,
    gbuf, pbuf, mom_t, mom, acc, crecv, xsend, xrecv, xlsend, xlrecv, ysum, ysend, yrecv, ylown, ylsend, zown, zrecv,
    yfsend, yfrecv, xfsum, xfrecv, gram, gcsend, gcrecv, gsum, gxsend, gxrecv, gfull,
    mrecv, pboth, dsend, dall, upd, ssend, syrecv, szrecv,
    lsem, send_sem, recv_sem,
):
    dp, tensor = lax.axis_index("dp"), lax.axis_index("tensor")
    zlo, y = dp // NY, dp % NY
    x, zhi, core = tensor // 4, (tensor // 2) % 2, tensor % 2
    z = zhi * NZLO + zlo
    other = 1 - core
    quarter = zhi * 2 + core

    def at(delta):
        dx, dy, dz, dk = delta
        px, py, pz, pk = (x + dx) % NX, (y + dy) % NY, (z + dz) % NZ, (core + dk) % 2
        return ((pz % NZLO) * NY + py, px * 4 + (pz // NZLO) * 2 + pk)

    started = {}

    def send(group, like, src, dst, delta):
        pltpu.make_async_remote_copy(
            src_ref=src, dst_ref=dst, send_sem=send_sem.at[group], recv_sem=recv_sem.at[group],
            device_id=at(delta), device_id_type=MESH,
        ).start()
        started[group] = like

    def arrived(group):
        like = started[group]
        pltpu.make_async_copy(like, like, recv_sem.at[group]).wait()

    def sent(groups):
        for group in groups:
            like = started[group]
            pltpu.make_async_copy(like, like, send_sem.at[group]).wait()

    loads = [pltpu.make_async_copy(projector, pbuf, lsem.at[0])]
    for s in range(NZLO):
        chunk = (zlo + OWNER[s]) % NZLO
        rows = pl.ds(pl.multiple_of(chunk * CHUNK, CHUNK), CHUNK)
        loads.append(pltpu.make_async_copy(grads.at[0, rows], gbuf.at[s], lsem.at[1 + s]))
    loads.append(pltpu.make_async_copy(first, mom_t.at[0], lsem.at[5]))
    loads.append(pltpu.make_async_copy(second, mom_t.at[1], lsem.at[6]))

    for load in loads[:2]:
        load.start()
    barrier = pltpu.get_barrier_semaphore()
    for delta in PARTNERS:
        pl.semaphore_signal(barrier, inc=1, device_id=at(delta), device_id_type=MESH)
    for load in loads[2:]:
        load.start()

    loads[0].wait()

    def core_send(s):
        send(G_CORE + s, crecv.at[s], acc.at[s, :, other], crecv.at[s], CORE[0])

    for s in range(NZLO):
        loads[1 + s].wait()
        out = jnp.dot(gbuf[s], pbuf[...], preferred_element_type=F32)
        acc[s] = out.reshape(NY, 2, HALF, COLS)
        if s == GREET:
            pl.semaphore_wait(barrier, len(PARTNERS))
            for t in range(s):
                core_send(t)
        if s >= GREET:
            core_send(s)

    def stacked(block):
        return jnp.concatenate([block[:, t * TILE:(t + 1) * TILE] for t in range(NX)], axis=0)

    def along_y_first():
        arrived(G_CORE + YF)
        for j, delta in enumerate(YS):
            there = (y + delta[1]) % NY
            yfsend[j] = stacked(acc[YF, there, core] + crecv[YF, there]).astype(BF16)
            send(G_YF, yfrecv, yfsend.at[j], yfrecv.at[j], delta)

    def along_x_first(s):
        i = XF.index(s)
        arrived(G_CORE + s)
        for j, delta in enumerate(XS):
            lanes = pl.ds(pl.multiple_of(((x + delta[0]) % NX) * TILE, TILE), TILE)
            tile = acc[s, :, core, :, lanes] + crecv[s, :, :, lanes]
            xsend[i, j] = tile.reshape(NY * HALF, TILE).astype(BF16)
            send(G_X + i, xrecv.at[i], xsend.at[i, j], xrecv.at[i, j], delta)

    def last_part(d, lanes):
        there = (y + d) % NY
        return acc[LAST, there, core, :, lanes] + crecv[LAST, there, :, lanes]

    def along_x_last(part):
        for j, delta in enumerate(XS):
            lanes = pl.ds(pl.multiple_of(((x + delta[0]) % NX) * TILE, TILE), TILE)
            block = jnp.concatenate([last_part(d, lanes) for d in PARTS[part]], axis=0)
            xlsend[part, j] = block.astype(BF16)
            send(G_XL + part, xlrecv.at[part], xlsend.at[part, j], xlrecv.at[part, j], delta)

    along_x_first(0)
    along_y_first()
    along_x_first(2)
    arrived(G_CORE + LAST)
    along_x_last(0)
    along_x_last(1)

    loads[5].wait()
    loads[6].wait()
    mom[0] = flip(mom_t[0])
    mom[1] = flip(mom_t[1])
    for j, delta in enumerate(HC):
        target_half = (core + delta[3]) % 2
        rows = pl.ds(pl.multiple_of(target_half * HALF, 8), HALF)
        send(G_M, mrecv.at[0:3], mom.at[:, rows], mrecv.at[quarter], delta)
    mrecv[quarter] = mom[:, pl.ds(pl.multiple_of(core * HALF, 8), HALF)]

    gram[...] = lax.dot_general(
        pbuf[...], pbuf[...], (((0,), (0,)), ((), ())), preferred_element_type=F32
    ).reshape(2, COLS // 2, COLS)
    gcsend[...] = gram[other].astype(BF16)
    send(G_GC, gcrecv, gcsend, gcrecv, CORE[0])

    def along_y(s):
        i = XF.index(s)
        arrived(G_X + i)
        lanes = pl.ds(pl.multiple_of(x * TILE, TILE), TILE)
        total = acc[s, :, core, :, lanes] + crecv[s, :, :, lanes]
        for j in range(len(XS)):
            total = total + xrecv[i, j].astype(F32).reshape(NY, HALF, TILE)
        ysum[i] = total
        padded = jnp.concatenate([total, jnp.zeros((NY, PADDED - HALF, TILE), F32)], axis=1)
        ysend[i] = padded.astype(BF16)
        for j, delta in enumerate(YS):
            send(G_Y + i, yrecv.at[i], ysend.at[i, (y + delta[1]) % NY], yrecv.at[i, j], delta)

    def along_x_after():
        total = stacked(acc[YF, y, core] + crecv[YF, y])
        arrived(G_YF)
        for j in range(len(YS)):
            total = total + yfrecv[j].astype(F32)
        xfsum[...] = total.reshape(NX, HALF, TILE)
        for j, delta in enumerate(XS):
            send(G_XF, xfrecv, xfsum.at[(x + delta[0]) % NX], xfrecv.at[j], delta)

    def along_y_last(part):
        lanes = pl.ds(pl.multiple_of(x * TILE, TILE), TILE)
        arrived(G_XL + part)
        others = xlrecv[part, 0].astype(F32)
        for j in range(1, len(XS)):
            others = others + xlrecv[part, j].astype(F32)
        for q, d in enumerate(PARTS[part]):
            total = last_part(d, lanes) + others[q * HALF:(q + 1) * HALF]
            if d == 0:
                ylown[...] = total
                continue
            j = YS.index((0, d, 0, 0))
            padded = jnp.concatenate([total, jnp.zeros((PADDED - HALF, TILE), F32)], axis=0)
            ylsend[j] = padded.astype(BF16)
            send(G_Y + 2, yrecv.at[2], ylsend.at[j], yrecv.at[2, j], YS[j])

    along_y(0)
    along_y(2)
    arrived(G_GC)
    gsum[...] = (gram[core] + gcrecv[...].astype(F32)).reshape(NX, STRIPE, COLS)
    for j, delta in enumerate(XS):
        gxsend[j] = gsum[(x + delta[0]) % NX].astype(BF16)
        send(G_GX, gxrecv, gxsend.at[j], gxrecv.at[j], delta)
    along_y_last(0)
    along_y_last(1)
    along_x_after()

    for s in range(NZLO):
        if s == YF:
            total = xfsum[x]
            arrived(G_XF)
            for j in range(len(XS)):
                total = total + xfrecv[j]
        else:
            i = 2 if s == LAST else XF.index(s)
            total = ylown[...] if s == LAST else ysum[i, y]
            arrived(G_Y + i)
            for j in range(len(YS)):
                total = total + yrecv[i, j, 0:HALF].astype(F32)
        zown[s] = total
        for d in (OWNER[s] + NZLO, OWNER[s]):
            if d > 0:
                send(G_Z, zrecv, zown.at[s], zrecv.at[d - 1], (0, 0, d, 0))

    stripe = gsum[x]
    arrived(G_GX)
    for j in range(len(XS)):
        stripe = stripe + gxrecv[j].astype(F32)
    gfull[core, x] = stripe.astype(BF16)
    for delta in XS:
        send(G_GA, gfull.at[core, 0:3], gfull.at[core, x], gfull.at[core, x], delta)

    arrived(G_M)
    m_first = jnp.concatenate([mrecv[q, 0] for q in range(4)], axis=1)
    m_second = jnp.concatenate([mrecv[q, 1] for q in range(4)], axis=1)
    total = zown[0]
    arrived(G_Z)
    for d in range(1, NZ):
        total = total + zrecv[d - 1]
    averaged = total * (1.0 / 32.0)

    def moments(old_first, old_second, mean):
        return 0.9 * old_first + 0.1 * mean, 0.999 * old_second + 0.001 * mean * mean

    f, v = moments(m_first, m_second, averaged)
    direction = f / (jnp.sqrt(v) + 1e-08)
    direction = jnp.concatenate([direction, jnp.zeros((8, TILE), F32)], axis=0).astype(BF16)
    dsend[...] = direction
    for delta in XC:
        send(G_D, dall.at[0:7], dsend, dall.at[core * NX + x], delta)
    pboth[core] = averaged
    send(G_P, pboth.at[core], pboth.at[core], pboth.at[core], CORE[0])
    dall[core * NX + x] = direction
    arrived(G_GA)
    send(G_GB, gfull.at[core], gfull.at[core], gfull.at[core], CORE[0])
    arrived(G_D)
    whole = jnp.concatenate(
        [jnp.concatenate([dall[k * NX + t] for t in range(NX)], axis=1) for k in range(2)], axis=0
    )
    arrived(G_GB)
    square = jnp.dot(whole, gfull[...].reshape(COLS, COLS), preferred_element_type=F32)
    square = square * whole.astype(F32)
    folded = square[0:8]
    for r in range(1, 8):
        folded = folded + square[8 * r:8 * r + 8]
    lanes_sum = folded[:, 0:TILE]
    for t in range(1, NX):
        lanes_sum = lanes_sum + folded[:, t * TILE:(t + 1) * TILE]
    total = jnp.sum(lanes_sum, axis=0, keepdims=True)

    for r, (group, deltas, box) in enumerate(((G_SY, YS, syrecv), (G_SZ, ZS, szrecv))):
        ssend[r] = total
        for j, delta in enumerate(deltas):
            send(group, box, ssend.at[r], box.at[j], delta)
        if r == 0:
            update = lax.dot_general(
                whole, pbuf[...], (((1,), (1,)), ((), ())), preferred_element_type=F32
            )
            upd[...] = jnp.concatenate([update[0:HALF], update[32:32 + HALF]], axis=0)
            arrived(G_P)
            pieces = []
            for k in range(2):
                mean = pboth[k]
                piece = mean[:, 0:32]
                for q in range(1, 4):
                    piece = jnp.where(quarter == q, mean[:, 32 * q:32 * q + 32], piece)
                pieces.append(piece)
            mean_t[...] = flip(jnp.concatenate(pieces, axis=0))
            sent(g for g in range(GROUPS) if g not in (G_SY, G_SZ))
        arrived(group)
        for j in range(len(deltas)):
            total = total + box[j]

    total_sq = jnp.maximum(jnp.sum(total, axis=1, keepdims=True), 0.0)
    entries = float(1536 * 16384)
    factor = jnp.minimum(1.0, 0.02 * entries**0.5 / (jnp.sqrt(total_sq) + 1e-06))
    step[...] = factor * upd[...]
    sent((G_SY, G_SZ))


def body(grads, projector, weight, first_moment, second_moment):
    sem = pltpu.SemaphoreType.DMA
    vm = pltpu.VMEM
    operands = (grads, projector, first_moment.T, second_moment.T)
    step, mean_t = pl.pallas_call(
        kernel,
        name="galore_step",
        out_shape=(
            jax.ShapeDtypeStruct((ROWS, DEPTH), F32),
            jax.ShapeDtypeStruct((32, ROWS), F32),
        ),
        in_specs=[pl.BlockSpec(memory_space=pltpu.HBM)] * 4,
        out_specs=(pl.BlockSpec(memory_space=pltpu.VMEM),) * 2,
        scratch_shapes=[
            vm((NZLO, CHUNK, DEPTH), BF16),
            vm((DEPTH, COLS), BF16),
            vm((2, 32, ROWS), F32),
            vm((2, ROWS, 32), F32),
            vm((NZLO, NY, 2, HALF, COLS), F32),
            vm((NZLO, NY, HALF, COLS), F32),
            vm((2, 3, NY * HALF, TILE), BF16),
            vm((2, 3, NY * HALF, TILE), BF16),
            vm((2, 3, NY * HALF // 2, TILE), BF16),
            vm((2, 3, NY * HALF // 2, TILE), BF16),
            vm((2, NY, HALF, TILE), F32),
            vm((2, NY, PADDED, TILE), BF16),
            vm((3, 7, PADDED, TILE), BF16),
            vm((HALF, TILE), F32),
            vm((7, PADDED, TILE), BF16),
            vm((NZLO, HALF, TILE), F32),
            vm((7, HALF, TILE), F32),
            vm((7, NX * HALF, TILE), BF16),
            vm((7, NX * HALF, TILE), BF16),
            vm((NX, HALF, TILE), F32),
            vm((3, HALF, TILE), F32),
            vm((2, COLS // 2, COLS), F32),
            vm((COLS // 2, COLS), BF16),
            vm((COLS // 2, COLS), BF16),
            vm((NX, STRIPE, COLS), F32),
            vm((3, STRIPE, COLS), BF16),
            vm((3, STRIPE, COLS), BF16),
            vm((2, NX, STRIPE, COLS), BF16),
            vm((4, 2, HALF, 32), F32),
            vm((2, HALF, TILE), F32),
            vm((32, TILE), BF16),
            vm((2 * NX, 32, TILE), BF16),
            vm((ROWS, DEPTH), F32),
            vm((2, 1, TILE), F32),
            vm((7, 1, TILE), F32),
            vm((7, 1, TILE), F32),
            sem((7,)),
            sem((GROUPS,)),
            sem((GROUPS,)),
        ],
        compiler_params=pltpu.CompilerParams(
            collective_id=0, has_side_effects=True, vmem_limit_bytes=48 * 2**20
        ),
    )(*(pltpu.with_memory_space_constraint(a, pltpu.HBM) for a in operands))
    mean = mean_t.T
    new_first = 0.9 * first_moment + 0.1 * mean
    new_second = 0.999 * second_moment + 0.001 * mean * mean
    return weight - step, new_first, new_second


def solution(mesh):
    placed = (
        P("dp", None, "tensor"),
        P("tensor", None),
        P("dp", "tensor"),
        P("dp", "tensor"),
        P("dp", "tensor"),
    )
    return jax.shard_map(
        body,
        mesh=mesh,
        in_specs=placed,
        out_specs=(P("dp", "tensor"), P("dp", "tensor"), P("dp", "tensor")),
        check_vma=False,
    )
```

time: 51.6 us -> 48.2 us (0.934)
  Pallas kernels: 49.4 us -> 45.9 us
    pallas_call x1, Pallas kernels: 49.4 us -> 45.9 us  [body(): pl.pallas_call(kernel, name='galore_step', out_shape=(jax.ShapeDtypeStruc...]
where the time goes in v4:
time: 48.2 us; the launch traced here: 47.9 us
  Pallas kernels  45.9 us (95%)
  other arithmetic  1.32 us (3%)
  between operations  0.67 us (1%)
    pallas_call x1, Pallas kernels, body(): pl.pallas_call(kernel, name='galore_step', out_shape=(jax.ShapeDtypeStruc...  45.9 us

profile of v4, /device:TPU:1, one launch (start us, length us, event | category | flops | bytes accessed | tf_op | source)
XLA Modules:
  0.0 47.9 jit_solution(10752317244819866196)
XLA Ops:
  0.6 0.0 copy-start.2
  0.6 0.0 copy-start.1
  0.7 0.0 copy-start
  0.7 45.9 %galore_step.1 = (f32[48,1024]{1,0:T(8,128)S(1)}, f32[32,48]{1,0:T(8,128)S(1)}) custom-call(bf16[1,1536,1024]{2,1,0:T(8,128)(2,1)} %grads.1, bf16[1024,512]{1,0:T(8,128)(2,1)} %projector.1, f32[32,48]{1,0:T(8,128)} %bitcast.7, f32[32,48]{1,0:T(8,128)} %bitcast.8), custom_call_target="tpu_custom_call" | custom-call | tf_op jit(solution)/shard_map/galore_step/pallas_call | solution.py:322
  46.5 0.0 copy-done
  46.6 0.7 %sub.3 = f32[48,1024]{1,0:T(8,128)} subtract(f32[48,1024]{1,0:T(8,128)S(1)} %copy-done, f32[48,1024]{1,0:T(8,128)S(1)} %get-tuple-element.5) | non-fusion elementwise | flops 49152 | bytes 589824 | tf_op jit(solution)/shard_map/sub | solution.py:379
  47.3 0.0 copy-done.2
  47.3 0.0 copy-done.1
  47.3 0.6 %fusion = (f32[48,32]{0,1:T(8,128)}, f32[48,32]{0,1:T(8,128)}) fusion(f32[32,48]{1,0:T(8,128)S(1)} %get-tuple-element.6, f32[48,32]{0,1:T(8,128)S(1)} %copy-done.2, f32[48,32]{0,1:T(8,128)S(1)} %copy-done.1), kind=kLoop, calls=%fused_computation.1 | loop fusion | flops 10752 | bytes 30720 | tf_op jit(solution)/shard_map/add | solution.py:378
Async XLA Ops:
  0.6 46.6 %copy-start.2 = (f32[48,32]{0,1:T(8,128)S(1)}, f32[48,32]{0,1:T(8,128)}, u32[]{:S(2)}) copy-start(f32[48,32]{0,1:T(8,128)} %param.9) | copy-start | bytes 18436
  0.6 46.6 %copy-start.1 = (f32[48,32]{0,1:T(8,128)S(1)}, f32[48,32]{0,1:T(8,128)}, u32[]{:S(2)}) copy-start(f32[48,32]{0,1:T(8,128)} %param.8) | copy-start | bytes 18436
  0.7 45.9 %copy-start = (f32[48,1024]{1,0:T(8,128)S(1)}, f32[48,1024]{1,0:T(8,128)}, u32[]{:S(2)}) copy-start(f32[48,1024]{1,0:T(8,128)} %param.7) | copy-start | bytes 589828

commit v5 on v4

--- a/solution.py
+++ b/solution.py
@@ -13,8 +13,8 @@
 DEPTH = 1024
 CHUNK = NY * ROWS
 
-G_CORE, G_X, G_XL, G_Y, G_Z, G_M, G_D, G_P, G_SY, G_SZ = 0, 4, 6, 8, 11, 12, 13, 14, 15, 16
-G_YF, G_XF, G_GC, G_GX, G_GA, G_GB, GROUPS = 17, 18, 19, 20, 21, 22, 23
+G_CORE, G_X, G_XL, G_Y, G_Z, G_M, G_D, G_P, G_S = 0, 4, 6, 8, 11, 12, 13, 14, 15
+G_YF, G_XF, G_GC, G_GX, G_GA, G_GB, GROUPS = 16, 17, 18, 19, 20, 21, 22
 GREET = 1
 YF = 1
 XF = (0, 2)
@@ -39,6 +39,7 @@
 YS = farthest_first([(0, d, 0, 0) for d in range(1, NY)])
 ZS = farthest_first([(0, 0, d, 0) for d in range(1, NZ)])
 XC = farthest_first([(d, 0, 0, k) for d in range(NX) for k in range(2) if (d, k) != (0, 0)])
+YZ = farthest_first([(0, a, b, 0) for a in range(NY) for b in range(NZ) if (a, b) != (0, 0)])
 HC = farthest_first([(0, 0, h, k) for h in (0, 4) for k in range(2) if (h, k) != (0, 0)])
 PARTNERS = farthest_first(dict.fromkeys(YS + ZS + HC + XC))
 
@@ -55,7 +56,7 @@
     step, mean_t,
     gbuf, pbuf, mom_t, mom, acc, crecv, xsend, xrecv, xlsend, xlrecv, ysum, ysend, yrecv, ylown, ylsend, zown, zrecv,
     yfsend, yfrecv, xfsum, xfrecv, gram, gcsend, gcrecv, gsum, gxsend, gxrecv, gfull,
-    mrecv, pboth, dsend, dall, upd, ssend, syrecv, szrecv,
+    mrecv, pboth, dsend, dall, upd, sown, sbox,
     lsem, send_sem, recv_sem,
 ):
     dp, tensor = lax.axis_index("dp"), lax.axis_index("tensor")
@@ -285,34 +286,31 @@
         lanes_sum = lanes_sum + folded[:, t * TILE:(t + 1) * TILE]
     total = jnp.sum(lanes_sum, axis=0, keepdims=True)
 
-    for r, (group, deltas, box) in enumerate(((G_SY, YS, syrecv), (G_SZ, ZS, szrecv))):
-        ssend[r] = total
-        for j, delta in enumerate(deltas):
-            send(group, box, ssend.at[r], box.at[j], delta)
-        if r == 0:
-            update = lax.dot_general(
-                whole, pbuf[...], (((1,), (1,)), ((), ())), preferred_element_type=F32
-            )
-            upd[...] = jnp.concatenate([update[0:HALF], update[32:32 + HALF]], axis=0)
-            arrived(G_P)
-            pieces = []
-            for k in range(2):
-                mean = pboth[k]
-                piece = mean[:, 0:32]
-                for q in range(1, 4):
-                    piece = jnp.where(quarter == q, mean[:, 32 * q:32 * q + 32], piece)
-                pieces.append(piece)
-            mean_t[...] = flip(jnp.concatenate(pieces, axis=0))
-            sent(g for g in range(GROUPS) if g not in (G_SY, G_SZ))
-        arrived(group)
-        for j in range(len(deltas)):
-            total = total + box[j]
+    sown[...] = total
+    for j, delta in enumerate(YZ):
+        send(G_S, sbox, sown, sbox.at[j], delta)
+    update = lax.dot_general(
+        whole, pbuf[...], (((1,), (1,)), ((), ())), preferred_element_type=F32
+    )
+    upd[...] = jnp.concatenate([update[0:HALF], update[32:32 + HALF]], axis=0)
+    arrived(G_P)
+    pieces = []
+    for k in range(2):
+        mean = pboth[k]
+        piece = mean[:, 0:32]
+        for q in range(1, 4):
+            piece = jnp.where(quarter == q, mean[:, 32 * q:32 * q + 32], piece)
+        pieces.append(piece)
+    mean_t[...] = flip(jnp.concatenate(pieces, axis=0))
+    sent(g for g in range(GROUPS) if g != G_S)
+    arrived(G_S)
+    total = total + jnp.sum(sbox[...], axis=0)
 
     total_sq = jnp.maximum(jnp.sum(total, axis=1, keepdims=True), 0.0)
     entries = float(1536 * 16384)
     factor = jnp.minimum(1.0, 0.02 * entries**0.5 / (jnp.sqrt(total_sq) + 1e-06))
     step[...] = factor * upd[...]
-    sent((G_SY, G_SZ))
+    sent((G_S,))
 
 
 def body(grads, projector, weight, first_moment, second_moment):
@@ -362,9 +360,8 @@
             vm((32, TILE), BF16),
             vm((2 * NX, 32, TILE), BF16),
             vm((ROWS, DEPTH), F32),
-            vm((2, 1, TILE), F32),
-            vm((7, 1, TILE), F32),
-            vm((7, 1, TILE), F32),
+            vm((1, TILE), F32),
+            vm((NY * NZ - 1, 1, TILE), F32),
             sem((7,)),
             sem((GROUPS,)),
             sem((GROUPS,)),

time: 48.2 us -> 46.8 us (0.971)
  Pallas kernels: 45.9 us -> 44.7 us
    pallas_call x1, Pallas kernels: 45.9 us -> 44.7 us  [body(): pl.pallas_call(kernel, name='galore_step', out_shape=(jax.ShapeDtypeStruc...]
where the time goes in v5:
time: 46.8 us; the launch traced here: 46.7 us
  Pallas kernels  44.7 us (96%)
  other arithmetic  1.32 us (3%)
  between operations  0.67 us (1%)
    pallas_call x1, Pallas kernels, body(): pl.pallas_call(kernel, name='galore_step', out_shape=(jax.ShapeDtypeStruc...  44.7 us

profile of v5, /device:TPU:1, one launch (start us, length us, event | category | flops | bytes accessed | tf_op | source)
XLA Modules:
  0.0 46.7 jit_solution(6665830106584776120)
XLA Ops:
  0.6 0.0 copy-start.2
  0.6 0.0 copy-start.1
  0.7 0.0 copy-start
  0.7 44.7 %galore_step.1 = (f32[48,1024]{1,0:T(8,128)S(1)}, f32[32,48]{1,0:T(8,128)S(1)}) custom-call(bf16[1,1536,1024]{2,1,0:T(8,128)(2,1)} %grads.1, bf16[1024,512]{1,0:T(8,128)(2,1)} %projector.1, f32[32,48]{1,0:T(8,128)} %bitcast.7, f32[32,48]{1,0:T(8,128)} %bitcast.8), custom_call_target="tpu_custom_call" | custom-call | tf_op jit(solution)/shard_map/galore_step/pallas_call | solution.py:320
  45.4 0.0 copy-done
  45.4 0.7 %sub.3 = f32[48,1024]{1,0:T(8,128)} subtract(f32[48,1024]{1,0:T(8,128)S(1)} %copy-done, f32[48,1024]{1,0:T(8,128)S(1)} %get-tuple-element.5) | non-fusion elementwise | flops 49152 | bytes 589824 | tf_op jit(solution)/shard_map/sub | solution.py:376
  46.1 0.0 copy-done.2
  46.1 0.0 copy-done.1
  46.1 0.6 %fusion = (f32[48,32]{0,1:T(8,128)}, f32[48,32]{0,1:T(8,128)}) fusion(f32[32,48]{1,0:T(8,128)S(1)} %get-tuple-element.6, f32[48,32]{0,1:T(8,128)S(1)} %copy-done.2, f32[48,32]{0,1:T(8,128)S(1)} %copy-done.1), kind=kLoop, calls=%fused_computation.1 | loop fusion | flops 10752 | bytes 30720 | tf_op jit(solution)/shard_map/add | solution.py:375
Async XLA Ops:
  0.6 45.4 %copy-start.2 = (f32[48,32]{0,1:T(8,128)S(1)}, f32[48,32]{0,1:T(8,128)}, u32[]{:S(2)}) copy-start(f32[48,32]{0,1:T(8,128)} %param.9) | copy-start | bytes 18436
  0.6 45.4 %copy-start.1 = (f32[48,32]{0,1:T(8,128)S(1)}, f32[48,32]{0,1:T(8,128)}, u32[]{:S(2)}) copy-start(f32[48,32]{0,1:T(8,128)} %param.8) | copy-start | bytes 18436
  0.7 44.7 %copy-start = (f32[48,1024]{1,0:T(8,128)S(1)}, f32[48,1024]{1,0:T(8,128)}, u32[]{:S(2)}) copy-start(f32[48,1024]{1,0:T(8,128)} %param.7) | copy-start | bytes 589828

commit v6 on v5

--- a/solution.py
+++ b/solution.py
@@ -13,14 +13,13 @@
 DEPTH = 1024
 CHUNK = NY * ROWS
 
-G_CORE, G_X, G_XL, G_Y, G_Z, G_M, G_D, G_P, G_S = 0, 4, 6, 8, 11, 12, 13, 14, 15
-G_YF, G_XF, G_GC, G_GX, G_GA, G_GB, GROUPS = 16, 17, 18, 19, 20, 21, 22
+G_CORE, G_X, G_Y, G_YF, G_Z, G_M, G_D, G_P, G_S = 0, 4, 8, 12, 16, 17, 18, 19, 20
+G_XF, G_GC, G_GX, G_GA, G_GB, GROUPS = 21, 22, 23, 24, 25, 26
 GREET = 1
-YF = 1
-XF = (0, 2)
 OWNER = (0, 1, 3, 2)
-LAST = NZLO - 1
-PARTS = ((4, 3, 5, 6), (2, 1, 7, 0))
+FAR = ((4, 3, 5, 6), (4, 5, 3, 2)) * 2
+NEAR = ((2, 1, 7), (6, 7, 1)) * 2
+BLOCKS = 4 * HALF
 STRIPE = 64
 PADDED = 32
 
@@ -54,8 +53,8 @@
 def kernel(
     grads, projector, first, second,
     step, mean_t,
-    gbuf, pbuf, mom_t, mom, acc, crecv, xsend, xrecv, xlsend, xlrecv, ysum, ysend, yrecv, ylown, ylsend, zown, zrecv,
-    yfsend, yfrecv, xfsum, xfrecv, gram, gcsend, gcrecv, gsum, gxsend, gxrecv, gfull,
+    gbuf, pbuf, mom_t, mom, acc, crecv, xsend, xrecv, ysend, yrecv, zown, zrecv,
+    yfsend, yfrecv, xfsum, xfsend, xfrecv, gram, gcsend, gcrecv, gsum, gxsend, gxrecv, gfull,
     mrecv, pboth, dsend, dall, upd, sown, sbox,
     lsem, send_sem, recv_sem,
 ):
@@ -124,39 +123,25 @@
     def stacked(block):
         return jnp.concatenate([block[:, t * TILE:(t + 1) * TILE] for t in range(NX)], axis=0)
 
-    def along_y_first():
-        arrived(G_CORE + YF)
-        for j, delta in enumerate(YS):
-            there = (y + delta[1]) % NY
-            yfsend[j] = stacked(acc[YF, there, core] + crecv[YF, there]).astype(BF16)
-            send(G_YF, yfrecv, yfsend.at[j], yfrecv.at[j], delta)
-
-    def along_x_first(s):
-        i = XF.index(s)
-        arrived(G_CORE + s)
+    def mine(s, d, lanes):
+        there = (y + d) % NY
+        return acc[s, there, core, :, lanes] + crecv[s, there, :, lanes]
+
+    def along_x(s):
         for j, delta in enumerate(XS):
             lanes = pl.ds(pl.multiple_of(((x + delta[0]) % NX) * TILE, TILE), TILE)
-            tile = acc[s, :, core, :, lanes] + crecv[s, :, :, lanes]
-            xsend[i, j] = tile.reshape(NY * HALF, TILE).astype(BF16)
-            send(G_X + i, xrecv.at[i], xsend.at[i, j], xrecv.at[i, j], delta)
-
-    def last_part(d, lanes):
-        there = (y + d) % NY
-        return acc[LAST, there, core, :, lanes] + crecv[LAST, there, :, lanes]
-
-    def along_x_last(part):
-        for j, delta in enumerate(XS):
-            lanes = pl.ds(pl.multiple_of(((x + delta[0]) % NX) * TILE, TILE), TILE)
-            block = jnp.concatenate([last_part(d, lanes) for d in PARTS[part]], axis=0)
-            xlsend[part, j] = block.astype(BF16)
-            send(G_XL + part, xlrecv.at[part], xlsend.at[part, j], xlrecv.at[part, j], delta)
-
-    along_x_first(0)
-    along_y_first()
-    along_x_first(2)
-    arrived(G_CORE + LAST)
-    along_x_last(0)
-    along_x_last(1)
+            xsend[s, j] = jnp.concatenate([mine(s, d, lanes) for d in FAR[s]], axis=0).astype(BF16)
+            send(G_X + s, xrecv.at[s], xsend.at[s, j], xrecv.at[s, j], delta)
+
+    def along_y_first(s):
+        for j, d in enumerate(NEAR[s]):
+            yfsend[s, j] = stacked(mine(s, d, slice(None))).astype(BF16)
+            send(G_YF + s, yfrecv.at[s], yfsend.at[s, j], yfrecv.at[s, j], (0, d, 0, 0))
+
+    for s in range(NZLO):
+        arrived(G_CORE + s)
+        along_x(s)
+        along_y_first(s)
 
     loads[5].wait()
     loads[6].wait()
@@ -175,66 +160,50 @@
     send(G_GC, gcrecv, gcsend, gcrecv, CORE[0])
 
     def along_y(s):
-        i = XF.index(s)
-        arrived(G_X + i)
+        arrived(G_X + s)
         lanes = pl.ds(pl.multiple_of(x * TILE, TILE), TILE)
-        total = acc[s, :, core, :, lanes] + crecv[s, :, :, lanes]
-        for j in range(len(XS)):
-            total = total + xrecv[i, j].astype(F32).reshape(NY, HALF, TILE)
-        ysum[i] = total
-        padded = jnp.concatenate([total, jnp.zeros((NY, PADDED - HALF, TILE), F32)], axis=1)
-        ysend[i] = padded.astype(BF16)
-        for j, delta in enumerate(YS):
-            send(G_Y + i, yrecv.at[i], ysend.at[i, (y + delta[1]) % NY], yrecv.at[i, j], delta)
-
-    def along_x_after():
-        total = stacked(acc[YF, y, core] + crecv[YF, y])
-        arrived(G_YF)
-        for j in range(len(YS)):
-            total = total + yfrecv[j].astype(F32)
-        xfsum[...] = total.reshape(NX, HALF, TILE)
-        for j, delta in enumerate(XS):
-            send(G_XF, xfrecv, xfsum.at[(x + delta[0]) % NX], xfrecv.at[j], delta)
-
-    def along_y_last(part):
-        lanes = pl.ds(pl.multiple_of(x * TILE, TILE), TILE)
-        arrived(G_XL + part)
-        others = xlrecv[part, 0].astype(F32)
+        others = xrecv[s, 0].astype(F32)
         for j in range(1, len(XS)):
-            others = others + xlrecv[part, j].astype(F32)
-        for q, d in enumerate(PARTS[part]):
-            total = last_part(d, lanes) + others[q * HALF:(q + 1) * HALF]
-            if d == 0:
-                ylown[...] = total
-                continue
-            j = YS.index((0, d, 0, 0))
+            others = others + xrecv[s, j].astype(F32)
+        for j, d in enumerate(FAR[s]):
+            total = mine(s, d, lanes) + others[j * HALF:(j + 1) * HALF]
             padded = jnp.concatenate([total, jnp.zeros((PADDED - HALF, TILE), F32)], axis=0)
-            ylsend[j] = padded.astype(BF16)
-            send(G_Y + 2, yrecv.at[2], ylsend.at[j], yrecv.at[2, j], YS[j])
+            ysend[s, j] = padded.astype(BF16)
+            send(G_Y + s, yrecv.at[s], ysend.at[s, j], yrecv.at[s, j], (0, d, 0, 0))
+
+    def gathered_along_y(s):
+        arrived(G_YF + s)
+        total = stacked(mine(s, 0, slice(None)))
+        for j in range(len(NEAR[s])):
+            total = total + yfrecv[s, j].astype(F32)
+        xfsum[:, s] = total.reshape(NX, HALF, TILE)
 
     along_y(0)
-    along_y(2)
+    gathered_along_y(0)
+    along_y(1)
+    gathered_along_y(1)
     arrived(G_GC)
     gsum[...] = (gram[core] + gcrecv[...].astype(F32)).reshape(NX, STRIPE, COLS)
     for j, delta in enumerate(XS):
         gxsend[j] = gsum[(x + delta[0]) % NX].astype(BF16)
         send(G_GX, gxrecv, gxsend.at[j], gxrecv.at[j], delta)
-    along_y_last(0)
-    along_y_last(1)
-    along_x_after()
-
+    along_y(2)
+    along_y(3)
+    gathered_along_y(2)
+    gathered_along_y(3)
+    for j, delta in enumerate(XS):
+        tile = xfsum[(x + delta[0]) % NX].reshape(BLOCKS, TILE)
+        xfsend[j] = tile.astype(BF16)
+        send(G_XF, xfrecv, xfsend.at[j], xfrecv.at[j], delta)
+
+    arrived(G_XF)
     for s in range(NZLO):
-        if s == YF:
-            total = xfsum[x]
-            arrived(G_XF)
-            for j in range(len(XS)):
-                total = total + xfrecv[j]
-        else:
-            i = 2 if s == LAST else XF.index(s)
-            total = ylown[...] if s == LAST else ysum[i, y]
-            arrived(G_Y + i)
-            for j in range(len(YS)):
-                total = total + yrecv[i, j, 0:HALF].astype(F32)
+        total = xfsum[x, s]
+        for j in range(len(XS)):
+            total = total + xfrecv[j].astype(F32)[s * HALF:(s + 1) * HALF]
+        arrived(G_Y + s)
+        for j in range(len(FAR[s])):
+            total = total + yrecv[s, j, 0:HALF].astype(F32)
         zown[s] = total
         for d in (OWNER[s] + NZLO, OWNER[s]):
             if d > 0:
@@ -333,21 +302,17 @@
             vm((2, ROWS, 32), F32),
             vm((NZLO, NY, 2, HALF, COLS), F32),
             vm((NZLO, NY, HALF, COLS), F32),
-            vm((2, 3, NY * HALF, TILE), BF16),
-            vm((2, 3, NY * HALF, TILE), BF16),
-            vm((2, 3, NY * HALF // 2, TILE), BF16),
-            vm((2, 3, NY * HALF // 2, TILE), BF16),
-            vm((2, NY, HALF, TILE), F32),
-            vm((2, NY, PADDED, TILE), BF16),
-            vm((3, 7, PADDED, TILE), BF16),
-            vm((HALF, TILE), F32),
-            vm((7, PADDED, TILE), BF16),
+            vm((NZLO, 3, BLOCKS, TILE), BF16),
+            vm((NZLO, 3, BLOCKS, TILE), BF16),
+            vm((NZLO, 4, PADDED, TILE), BF16),
+            vm((NZLO, 4, PADDED, TILE), BF16),
             vm((NZLO, HALF, TILE), F32),
             vm((7, HALF, TILE), F32),
-            vm((7, NX * HALF, TILE), BF16),
-            vm((7, NX * HALF, TILE), BF16),
-            vm((NX, HALF, TILE), F32),
-            vm((3, HALF, TILE), F32),
+            vm((NZLO, 3, NX * HALF, TILE), BF16),
+            vm((NZLO, 3, NX * HALF, TILE), BF16),
+            vm((NX, NZLO, HALF, TILE), F32),
+            vm((3, BLOCKS, TILE), BF16),
+            vm((3, BLOCKS, TILE), BF16),
             vm((2, COLS // 2, COLS), F32),
             vm((COLS // 2, COLS), BF16),
             vm((COLS // 2, COLS), BF16),

time: 46.8 us -> 45.7 us (0.976)
  Pallas kernels: 44.7 us -> 43.5 us
    pallas_call x1, Pallas kernels: 44.7 us -> 43.5 us  [body(): pl.pallas_call(kernel, name='galore_step', out_shape=(jax.ShapeDtypeStruc...]
where the time goes in v6:
time: 45.7 us; the launch traced here: 45.5 us
  Pallas kernels  43.5 us (95%)
  other arithmetic  1.32 us (3%)
  between operations  0.67 us (1%)
    pallas_call x1, Pallas kernels, body(): pl.pallas_call(kernel, name='galore_step', out_shape=(jax.ShapeDtypeStruc...  43.5 us

profile of v6, /device:TPU:1, one launch (start us, length us, event | category | flops | bytes accessed | tf_op | source)
XLA Modules:
  0.0 45.5 jit_solution(2426784884011184781)
XLA Ops:
  0.6 0.0 copy-start.2
  0.6 0.0 copy-start.1
  0.7 0.0 copy-start
  0.7 43.5 %galore_step.1 = (f32[48,1024]{1,0:T(8,128)S(1)}, f32[32,48]{1,0:T(8,128)S(1)}) custom-call(bf16[1,1536,1024]{2,1,0:T(8,128)(2,1)} %grads.1, bf16[1024,512]{1,0:T(8,128)(2,1)} %projector.1, f32[32,48]{1,0:T(8,128)} %bitcast.7, f32[32,48]{1,0:T(8,128)} %bitcast.8), custom_call_target="tpu_custom_call" | custom-call | tf_op jit(solution)/shard_map/galore_step/pallas_call | solution.py:289
  44.2 0.0 copy-done
  44.2 0.7 %sub.3 = f32[48,1024]{1,0:T(8,128)} subtract(f32[48,1024]{1,0:T(8,128)S(1)} %copy-done, f32[48,1024]{1,0:T(8,128)S(1)} %get-tuple-element.5) | non-fusion elementwise | flops 49152 | bytes 589824 | tf_op jit(solution)/shard_map/sub | solution.py:341
  44.9 0.0 copy-done.2
  44.9 0.0 copy-done.1
  44.9 0.6 %fusion = (f32[48,32]{0,1:T(8,128)}, f32[48,32]{0,1:T(8,128)}) fusion(f32[32,48]{1,0:T(8,128)S(1)} %get-tuple-element.6, f32[48,32]{0,1:T(8,128)S(1)} %copy-done.2, f32[48,32]{0,1:T(8,128)S(1)} %copy-done.1), kind=kLoop, calls=%fused_computation.1 | loop fusion | flops 10752 | bytes 30720 | tf_op jit(solution)/shard_map/add | solution.py:340
Async XLA Ops:
  0.6 44.3 %copy-start.2 = (f32[48,32]{0,1:T(8,128)S(1)}, f32[48,32]{0,1:T(8,128)}, u32[]{:S(2)}) copy-start(f32[48,32]{0,1:T(8,128)} %param.9) | copy-start | bytes 18436
  0.6 44.3 %copy-start.1 = (f32[48,32]{0,1:T(8,128)S(1)}, f32[48,32]{0,1:T(8,128)}, u32[]{:S(2)}) copy-start(f32[48,32]{0,1:T(8,128)} %param.8) | copy-start | bytes 18436
  0.7 43.6 %copy-start = (f32[48,1024]{1,0:T(8,128)S(1)}, f32[48,1024]{1,0:T(8,128)}, u32[]{:S(2)}) copy-start(f32[48,1024]{1,0:T(8,128)} %param.7) | copy-start | bytes 589828

commit v7 on v6

--- a/solution.py
+++ b/solution.py
@@ -14,7 +14,7 @@
 CHUNK = NY * ROWS
 
 G_CORE, G_X, G_Y, G_YF, G_Z, G_M, G_D, G_P, G_S = 0, 4, 8, 12, 16, 17, 18, 19, 20
-G_XF, G_GC, G_GX, G_GA, G_GB, GROUPS = 21, 22, 23, 24, 25, 26
+G_XF, G_GC, G_GX, G_GA, G_GB, GROUPS = 21, 23, 24, 25, 26, 27
 GREET = 1
 OWNER = (0, 1, 3, 2)
 FAR = ((4, 3, 5, 6), (4, 5, 3, 2)) * 2
@@ -178,10 +178,17 @@
             total = total + yfrecv[s, j].astype(F32)
         xfsum[:, s] = total.reshape(NX, HALF, TILE)
 
+    def along_x_after(half):
+        for j, delta in enumerate(XS):
+            tile = xfsum[(x + delta[0]) % NX, 2 * half:2 * half + 2].reshape(2 * HALF, TILE)
+            xfsend[half, j] = tile.astype(BF16)
+            send(G_XF + half, xfrecv.at[half], xfsend.at[half, j], xfrecv.at[half, j], delta)
+
     along_y(0)
     gathered_along_y(0)
     along_y(1)
     gathered_along_y(1)
+    along_x_after(0)
     arrived(G_GC)
     gsum[...] = (gram[core] + gcrecv[...].astype(F32)).reshape(NX, STRIPE, COLS)
     for j, delta in enumerate(XS):
@@ -191,16 +198,15 @@
     along_y(3)
     gathered_along_y(2)
     gathered_along_y(3)
-    for j, delta in enumerate(XS):
-        tile = xfsum[(x + delta[0]) % NX].reshape(BLOCKS, TILE)
-        xfsend[j] = tile.astype(BF16)
-        send(G_XF, xfrecv, xfsend.at[j], xfrecv.at[j], delta)
-
-    arrived(G_XF)
+    along_x_after(1)
+
     for s in range(NZLO):
+        half, row = s // 2, s % 2 * HALF
+        if s % 2 == 0:
+            arrived(G_XF + half)
         total = xfsum[x, s]
         for j in range(len(XS)):
-            total = total + xfrecv[j].astype(F32)[s * HALF:(s + 1) * HALF]
+            total = total + xfrecv[half, j].astype(F32)[row:row + HALF]
         arrived(G_Y + s)
         for j in range(len(FAR[s])):
             total = total + yrecv[s, j, 0:HALF].astype(F32)
@@ -311,8 +317,8 @@
             vm((NZLO, 3, NX * HALF, TILE), BF16),
             vm((NZLO, 3, NX * HALF, TILE), BF16),
             vm((NX, NZLO, HALF, TILE), F32),
-            vm((3, BLOCKS, TILE), BF16),
-            vm((3, BLOCKS, TILE), BF16),
+            vm((2, 3, 2 * HALF, TILE), BF16),
+            vm((2, 3, 2 * HALF, TILE), BF16),
             vm((2, COLS // 2, COLS), F32),
             vm((COLS // 2, COLS), BF16),
             vm((COLS // 2, COLS), BF16),

time: 45.7 us -> 45.2 us (0.989)
  no operation moved by 1% of the time
where the time goes in v7:
time: 45.2 us; the launch traced here: 45.1 us
  Pallas kernels  43.1 us (95%)
  other arithmetic  1.32 us (3%)
  between operations  0.67 us (1%)
    pallas_call x1, Pallas kernels, body(): pl.pallas_call(kernel, name='galore_step', out_shape=(jax.ShapeDtypeStruc...  43.1 us

profile of v7, /device:TPU:1, one launch (start us, length us, event | category | flops | bytes accessed | tf_op | source)
XLA Modules:
  0.0 45.1 jit_solution(11668670933135474868)
XLA Ops:
  0.6 0.0 copy-start.2
  0.6 0.0 copy-start.1
  0.7 0.0 copy-start
  0.7 43.1 %galore_step.1 = (f32[48,1024]{1,0:T(8,128)S(1)}, f32[32,48]{1,0:T(8,128)S(1)}) custom-call(bf16[1,1536,1024]{2,1,0:T(8,128)(2,1)} %grads.1, bf16[1024,512]{1,0:T(8,128)(2,1)} %projector.1, f32[32,48]{1,0:T(8,128)} %bitcast.7, f32[32,48]{1,0:T(8,128)} %bitcast.8), custom_call_target="tpu_custom_call" | custom-call | tf_op jit(solution)/shard_map/galore_step/pallas_call | solution.py:295
  43.8 0.0 copy-done
  43.8 0.7 %sub.3 = f32[48,1024]{1,0:T(8,128)} subtract(f32[48,1024]{1,0:T(8,128)S(1)} %copy-done, f32[48,1024]{1,0:T(8,128)S(1)} %get-tuple-element.5) | non-fusion elementwise | flops 49152 | bytes 589824 | tf_op jit(solution)/shard_map/sub | solution.py:347
  44.5 0.0 copy-done.2
  44.5 0.0 copy-done.1
  44.5 0.6 %fusion = (f32[48,32]{0,1:T(8,128)}, f32[48,32]{0,1:T(8,128)}) fusion(f32[32,48]{1,0:T(8,128)S(1)} %get-tuple-element.6, f32[48,32]{0,1:T(8,128)S(1)} %copy-done.2, f32[48,32]{0,1:T(8,128)S(1)} %copy-done.1), kind=kLoop, calls=%fused_computation.1 | loop fusion | flops 10752 | bytes 30720 | tf_op jit(solution)/shard_map/add | solution.py:346
Async XLA Ops:
  0.6 43.9 %copy-start.2 = (f32[48,32]{0,1:T(8,128)S(1)}, f32[48,32]{0,1:T(8,128)}, u32[]{:S(2)}) copy-start(f32[48,32]{0,1:T(8,128)} %param.9) | copy-start | bytes 18436
  0.6 43.9 %copy-start.1 = (f32[48,32]{0,1:T(8,128)S(1)}, f32[48,32]{0,1:T(8,128)}, u32[]{:S(2)}) copy-start(f32[48,32]{0,1:T(8,128)} %param.8) | copy-start | bytes 18436
  0.7 43.1 %copy-start = (f32[48,1024]{1,0:T(8,128)S(1)}, f32[48,1024]{1,0:T(8,128)}, u32[]{:S(2)}) copy-start(f32[48,1024]{1,0:T(8,128)} %param.7) | copy-start | bytes 589828
